TPU v7x, 32 devices: a whole 2x2x4 slice. The times are simulated.
32 devices in a mesh: groups: 2 (over x), scen: 16 (over z, y, core).
Axes of the slice: x: 2, y: 2, z: 4, core: 2. Of those that a mesh axis runs over, the one named last changes fastest.
Arguments:
- factors: bfloat16 [512, 1024], P(('groups', 'scen')), parts along dimension 0, may hold values from -6 to 6
- loadings: bfloat16 [65536, 512], P(('groups', 'scen')), parts along dimension 0, may hold values from -6 to 6
- pattern: int32 [512, 4], P(('groups', 'scen')), parts along dimension 0, may hold values from 0 to 7, as said below
- threshold: float32 [65536], P(('groups', 'scen')), parts along dimension 0, may hold values from -3 to -1
- rho: float32 [65536], P(('groups', 'scen')), parts along dimension 0, may hold values from 0.1 to 0.5
- exposure: float32 [65536], P(('groups', 'scen')), parts along dimension 0, may hold values from 1 to 30
- region: int32 [65536], P(('groups', 'scen')), parts along dimension 0, may hold values from 0 to 15
- tail_mask: int32 [512], P('groups'), parts along dimension 0, may hold values from 0 to 1, as said below
- var_index: int32 [2], P('groups'), parts along dimension 0, may hold values from 0 to 255
Outputs:
- region_loss: float32 [16, 512], P(None, ('groups', 'scen')), parts along dimension 1
- contributions: float32 [65536], P(('groups', 'scen')), parts along dimension 0
- var_contributions: float32 [65536], P(('groups', 'scen')), parts along dimension 0
There are 2 independent parts, one for each index of `groups`. A program takes and returns all parts, laid end to end along the dimension named above; each array names one. Nothing has to cross between parts.
Inputs may be any that keep to these rules, and one draw needn't show every extreme that they name: `pattern`: each row names 4 different factor blocks. `tail_mask`: exactly 16 scenarios are marked.
All inputs are finite; a program needn't handle non-finite values.
Results may differ from a plain program's by a relative error of at most 0.0003.
Values may be sent and summed in bfloat16 or wider, within the bound.
No kernel may reach another device: no remote copies, remote signals or barrier semaphores. Data moves between devices by JAX's collectives and lax.ppermute only.
A program may use at most 128 MiB of HBM per device.

v0:
```python
import jax
import jax.numpy as jnp
from jax import lax
from jax.sharding import PartitionSpec as P

R = 16


def slot_scores(loadings, pattern, factor_rows):
    member_count = loadings.shape[0] // 128
    number_of_openings = loadings.shape[1] // 128
    rows = factor_rows.shape[0]
    loading_block_list = loadings.reshape(member_count, 128, number_of_openings, 128)
    pieces = factor_rows.reshape(rows, factor_rows.shape[1] // 128, 128)
    total = jnp.zeros((member_count, 128, rows), jnp.float32)
    for opening_position in range(number_of_openings):
        chosen = jnp.take(pieces, pattern[:, opening_position], axis=1)
        total = total + jnp.einsum(
            "bok,pbk->bop",
            loading_block_list[:, :, opening_position, :],
            chosen,
            preferred_element_type=jnp.float32,
        )
    return total.reshape(member_count * 128, rows)


def local(factors, loadings, pattern, threshold, rho, exposure, region, tail_mask, var_index):
    local_rows = loadings.shape[0]
    block_width = loadings.shape[1]
    scen_local = factors.shape[0]
    scen_total = scen_local * lax.axis_size("scen")
    tail_count = scen_total // 16
    obligors_all = local_rows * lax.axis_size("scen")
    squares = loadings.astype(jnp.float32)
    mean_sq = jnp.mean(squares * squares, axis=1)
    loading_scale = jnp.sqrt(rho / (block_width * (mean_sq + 1e-06)))
    idio_scale = jnp.sqrt(1.0 - rho)
    root_two = jnp.sqrt(jnp.float32(2.0))
    onehot = (region[None, :] == jnp.arange(R, dtype=jnp.int32)[:, None]).astype(jnp.float32)
    ranks = jnp.cumsum(tail_mask) - 1
    picked = (tail_mask[:, None] == 1) & (
        ranks[:, None] == jnp.arange(tail_count, dtype=jnp.int32)[None, :]
    )
    var_column = (jnp.arange(scen_total, dtype=jnp.int32) == var_index[0])[:, None]
    selector = jnp.concatenate([picked, var_column], axis=1).astype(jnp.float32)
    score = slot_scores(loadings, pattern, lax.all_gather(factors, "scen", axis=0, tiled=True))
    argument = (threshold[:, None] - loading_scale[:, None] * score) / idio_scale[:, None]
    probs = 0.5 * jax.scipy.special.erfc(-argument / root_two)
    losses = jnp.dot(onehot, exposure[:, None] * probs, precision=lax.Precision.HIGHEST) * (
        R / obligors_all
    )
    kept = jnp.dot(probs, selector, precision=lax.Precision.HIGHEST)
    summed = lax.psum(losses, "scen")
    own_loss = lax.dynamic_slice_in_dim(summed, lax.axis_index("scen") * scen_local, scen_local, 1)
    contributions = exposure * jnp.mean(kept[:, :tail_count], axis=1)
    var_contributions = exposure * kept[:, tail_count]
    return (own_loss, contributions, var_contributions)


def solution(mesh):
    return jax.shard_map(
        local,
        mesh=mesh,
        in_specs=(
            P(("groups", "scen"), None),
            P(("groups", "scen"), None),
            P(("groups", "scen"), None),
            P(("groups", "scen")),
            P(("groups", "scen")),
            P(("groups", "scen")),
            P(("groups", "scen")),
            P("groups"),
            P("groups"),
        ),
        out_specs=(P(None, ("groups", "scen")), P(("groups", "scen")), P(("groups", "scen"))),
        check_vma=False,
    )
```

profile of v0, /device:TPU:0, one launch (start us, length us, event | category | flops | bytes accessed | tf_op | source)
XLA Modules:
  0.0 121.1 jit_solution(5535378209924065022)
XLA Ops:
  0.6 0.8 compare_and_fusion
  1.5 24.8 %all_gather.3 = bf16[256,1024]{1,0:T(8,128)(2,1)S(1)} all-gather(bf16[16,1024]{1,0:T(8,128)(2,1)} %param.11), channel_id=1, replica_groups=mesh['groups'=2,'scen'=16] {'scen'}, dimensions={0}, use_global_device_ids=true | all-gather | bytes 557056 | tf_op jit(solution)/shard_map/all_gather | solution.py:46
  26.3 0.2 copy.27
  26.5 0.3 copy.28
  26.8 1.7 %gather_fusion.1 = bf16[16,256,128]{2,1,0:T(8,128)(2,1)} fusion(bf16[256,8,128]{2,0,1:T(8,128)(2,1)S(1)} %copy.28, s32[1024]{0:T(1024)S(1)} %get-tuple-element.29), kind=kCustom, calls=%fused_computation.1.clone | custom fusion | bytes 2097216 | tf_op jit(solution)/shard_map/jit(_take)/gather | solution.py:17
  28.4 2.5 %reshape.109 = bf16[16,128,4,128]{3,2,1,0:T(4,128)(2,1)S(1)} reshape(bf16[2048,512]{1,0:T(8,128)(2,1)} %param.12) | data formatting | bytes 4194304 | tf_op jit(solution)/shard_map/reshape | solution.py:13
  31.0 0.0 copy-start.1
  31.0 5.5 %fusion.50 = (bf16[16,128,1,128]{3,2,1,0:T(2,128)(2,1)}, bf16[16,128,1,128]{3,2,1,0:T(2,128)(2,1)}, bf16[16,128,1,128]{3,2,1,0:T(2,128)(2,1)S(1)}, bf16[16,128,1,128]{3,2,1,0:T(2,128)(2,1)}) fusion(bf16[16,128,4,128]{3,2,1,0:T(4,128)(2,1)S(1)} %reshape.109), kind=kLoop, calls=%fused_computation.91 | loop fusion | bytes 4194304 | tf_op jit(solution)/shard_map/slice | solution.py:20
  36.4 0.0 copy-done.1
  36.5 0.5 fusion.21
  37.0 1.7 %gather_fusion = bf16[16,256,128]{2,1,0:T(8,128)(2,1)} fusion(bf16[256,8,128]{2,0,1:T(8,128)(2,1)S(1)} %copy.28, s32[1024]{0:T(1024)S(1)} %get-tuple-element.30), kind=kCustom, calls=%fused_computation.clone | custom fusion | bytes 2097216 | tf_op jit(solution)/shard_map/jit(_take)/gather | solution.py:17
  38.6 3.4 %fusion.23 = f32[16,256,128]{1,2,0:T(8,128)} fusion(bf16[16,256,128]{2,1,0:T(8,128)(2,1)} %gather_fusion, pred[16]{0:T(512)(128)(4,1)S(1)} %get-tuple-element.23, bf16[16,128,1,128]{3,2,1,0:T(2,128)(2,1)} %get-tuple-element.15), kind=kOutput, calls=%fused_computation.36 | convolution fusion | flops 134742016 | bytes 3670032 | tf_op jit(solution)/shard_map/bok,pbk->bop/dot_general | solution.py:18
  42.1 1.7 %gather_fusion.2 = bf16[16,256,128]{2,1,0:T(8,128)(2,1)} fusion(bf16[256,8,128]{2,0,1:T(8,128)(2,1)S(1)} %copy.28, s32[1024]{0:T(1024)S(1)} %get-tuple-element.28), kind=kCustom, calls=%fused_computation.2.clone | custom fusion | bytes 2097216 | tf_op jit(solution)/shard_map/jit(_take)/gather | solution.py:17
  43.7 3.4 %fusion.19 = f32[16,256,128]{1,2,0:T(8,128)} fusion(bf16[16,256,128]{2,1,0:T(8,128)(2,1)} %gather_fusion.2, pred[16]{0:T(512)(128)(4,1)S(1)} %get-tuple-element.25, bf16[16,128,1,128]{3,2,1,0:T(2,128)(2,1)} %get-tuple-element.13), kind=kOutput, calls=%fused_computation.32 | convolution fusion | flops 134742016 | bytes 3670032 | tf_op jit(solution)/shard_map/bok,pbk->bop/dot_general | solution.py:18
  47.1 1.7 %gather_fusion.3 = bf16[16,256,128]{2,1,0:T(8,128)(2,1)} fusion(bf16[256,8,128]{2,0,1:T(8,128)(2,1)S(1)} %copy.28, s32[1024]{0:T(1024)S(1)} %get-tuple-element.27), kind=kCustom, calls=%fused_computation.3.clone | custom fusion | bytes 2097216 | tf_op jit(solution)/shard_map/jit(_take)/gather | solution.py:17
  48.8 0.0 copy-start
  48.8 3.6 %add_add_fusion = f32[16,256,128]{1,2,0:T(8,128)S(1)} fusion(f32[16,256,128]{1,2,0:T(8,128)} %fusion.19, f32[16,256,128]{1,2,0:T(8,128)} %fusion.23, f32[16,256,128]{1,2,0:T(8,128)S(1)} %fusion.21, bf16[16,256,128]{2,1,0:T(8,128)(2,1)} %gather_fusion.3, pred[16]{0:T(512)(128)(4,1)S(1)} %get-tuple-element.4, bf16[16,128,1,128]{3,2,1,0:T(2,128)(2,1)} %get-tuple-element.12), kind=kOutput, calls=%fused_computation.28 | convolution fusion | flops 136314880 | bytes 9961488 | tf_op jit(solution)/shard_map/bok,pbk->bop/dot_general | solution.py:18
  52.4 0.0 copy-done
  52.4 0.0 copy-start.4
  52.4 0.0 copy-start.2
  52.4 0.5 multiply_reduce_fusion
  52.9 0.2 copy-done.4
  53.1 0.0 copy-done.2
  53.1 0.0 copy-start.6
  53.1 5.4 %fusion = f32[2048,256]{1,0:T(8,128)S(1)} fusion(f32[16,256,128]{1,2,0:T(8,128)S(1)} %add_add_fusion, f32[2048]{0:T(1024)S(1)} %get-tuple-element.20, f32[2048]{0:T(1024)S(1)} %get-tuple-element.19, f32[2048]{0:T(1024)S(1)} %copy-done.2), kind=kLoop, calls=%fused_computation.6 | loop fusion | flops 34078720 | bytes 4218880 | tf_op jit(solution)/shard_map/erfc | solution.py:48
  58.5 0.0 copy-start.5
  58.5 0.0 copy-start.3
  58.6 0.0 copy-done.6
  58.6 0.3 reduce-window.9
  58.9 0.1 slice.45
  59.0 0.1 slice_reduce_fusion.1
  59.1 0.1 add_bitcast_fusion
  59.9 1.1 fusion.5
  61.0 0.0 copy-done.5
  61.0 0.6 fusion.51
  61.6 0.0 copy-done.3
  61.6 0.9 fusion.15
  62.6 57.8 %psum.7 = f32[16,256]{1,0:T(8,128)S(1)} all-reduce(f32[16,256]{1,0:T(8,128)S(1)} %fusion.15), channel_id=1, replica_groups=mesh['groups'=2,'scen'=16] {'scen'}, use_global_device_ids=true, to_apply=%region_1.3 | all-reduce | flops 4096 | bytes 32768 | tf_op jit(solution)/shard_map/psum | solution.py:53
  120.4 0.7 constant_dynamic-slice_fusion
  (9 shorter events, 0.1 us)
Async XLA Ops:
  31.0 5.5 %copy-start.1 = (bf16[16,256,128]{2,1,0:T(8,128)(2,1)S(1)}, bf16[16,256,128]{2,1,0:T(8,128)(2,1)}, u32[]{:S(2)}) copy-start(bf16[16,256,128]{2,1,0:T(8,128)(2,1)} %gather_fusion.1) | copy-start | bytes 3145732
  48.8 3.6 %copy-start = (bf16[2048,512]{1,0:T(8,128)(2,1)S(1)}, bf16[2048,512]{1,0:T(8,128)(2,1)}, u32[]{:S(2)}) copy-start(bf16[2048,512]{1,0:T(8,128)(2,1)} %param.12) | copy-start | bytes 6291460
  52.4 0.7 copy-start.4
  52.4 0.7 copy-start.2
  53.1 5.4 %copy-start.6 = (s32[256]{0:T(256)S(1)}, s32[256]{0:T(256)}, u32[]{:S(2)}) copy-start(s32[256]{0:T(256)} %param.18) | copy-start | bytes 3076
  58.5 2.5 %copy-start.5 = (f32[2048]{0:T(1024)S(1)}, f32[2048]{0:T(1024)}, u32[]{:S(2)}) copy-start(f32[2048]{0:T(1024)} %param.16) | copy-start | bytes 24580
  58.5 3.1 %copy-start.3 = (s32[2048]{0:T(1024)S(1)}, s32[2048]{0:T(1024)}, u32[]{:S(2)}) copy-start(s32[2048]{0:T(1024)} %param.17) | copy-start | bytes 24580
where the time goes:
time: 121 us
  blocking collectives  82.6 us (68%)
  local copies, waits for them, and re-layouts  16.3 us (13%)
  matrix products  12.9 us (11%)
  other arithmetic  7.81 us (6%)
  between operations  1.46 us (1%)
    psum x1, blocking collectives, local(): summed = lax.psum(losses, 'scen')  57.8 us
    all_gather x1, blocking collectives, local(): lax.all_gather(factors, 'scen', axis=0, tiled=True)  24.8 us
    dot_general x4, matrix products, slot_scores(): jnp.einsum('bok,pbk->bop', loading_block_list[:, :, opening_position, :],...  10.9 us
    gather x4, local copies, waits for them, and re-layouts, slot_scores(): chosen = jnp.take(pieces, pattern[:, opening_position], axis=1)  6.71 us
    slice x1, local copies, waits for them, and re-layouts, slot_scores(): loading_block_list[:, :, opening_position, :]  5.45 us
    another operation x1, other arithmetic, local(): probs = 0.5 * jax.scipy.special.erfc(-argument / root_two)  5.39 us
    reshape x1, local copies, waits for them, and re-layouts, slot_scores(): loadings.reshape(member_count, 128, number_of_openings, 128)  2.55 us

commit v1 on v0

v1 whole, which is shorter than its diff:
```python
import functools
import math

import jax
import jax.numpy as jnp
from jax import lax
from jax.experimental import pallas as pl
from jax.experimental.pallas import tpu as pltpu
from jax.sharding import PartitionSpec as P

R = 16
BLK = 128
NT = (((1,), (1,)), ((), ()))
TO_U = math.sqrt(math.log2(math.e) / 2.0)
SHIFT = 3.0
Q = (
    0.3388303816318512,
    1.0164676904678345,
    2.8077750205993652,
    6.835119247436523,
    17.085220336914062,
    -1.4560075998306274,
    182.0042724609375,
    -596.1250610351562,
    493.3643493652344,
)


def flipped(p, n):
    out = 0
    step = 1
    while step < n:
        out = 2 * out + (p & 1)
        p //= 2
        step *= 2
    return out


def prepare_kernel(load_ref, thr_ref, rho_ref, expo_ref, region_ref, par_ref, where_ref):
    rows = load_ref.shape[0]
    width = load_ref.shape[1]
    diagonal = lax.broadcasted_iota(jnp.int32, (BLK, BLK), 0) == lax.broadcasted_iota(jnp.int32, (BLK, BLK), 1)
    row_region = lax.broadcasted_iota(jnp.int32, (BLK, BLK), 0) % R
    for b in range(rows // BLK):
        at = slice(b * BLK, (b + 1) * BLK)
        block = load_ref[at, :]
        gram = lax.dot_general(block, block, NT, preferred_element_type=jnp.float32)
        mean_sq = jnp.sum(jnp.where(diagonal, gram, 0.0), axis=0, keepdims=True) * (1.0 / width)
        rho = rho_ref[:, at]
        scale = jnp.sqrt(rho / (width * (mean_sq + 1e-06)))
        to_u = TO_U / jnp.sqrt(1.0 - rho)
        par_ref[0:1, at] = -thr_ref[:, at] * to_u
        par_ref[1:2, at] = scale * to_u
        par_ref[2:3, at] = expo_ref[:, at]
        where_ref[:, at] = (row_region == region_ref[:, at]).astype(jnp.bfloat16)


def prepare(loadings, threshold, rho, exposure, region):
    rows = loadings.shape[0]
    return pl.pallas_call(
        prepare_kernel,
        out_shape=(
            jax.ShapeDtypeStruct((8, rows), jnp.float32),
            jax.ShapeDtypeStruct((BLK, rows), jnp.bfloat16),
        ),
        compiler_params=pltpu.CompilerParams(vmem_limit_bytes=24 << 20),
        cost_estimate=pl.CostEstimate(
            flops=2 * rows * BLK * loadings.shape[1], bytes_accessed=3 * rows * 512, transcendentals=2 * rows
        ),
        name="prepare",
    )(loadings, threshold[None], rho[None], exposure[None], region[None])


def losses_kernel(n, pat_ref, var_ref, own_ref, other_ref, load_ref, par_ref, where_ref, tail_ref, loss_ref, con_ref, varc_ref, fac_ref, acc_ref):
    me = lax.axis_index("scen")
    half = own_ref.shape[0]
    scen = 2 * half
    mine = scen // n
    for p in range(n):
        to = pl.multiple_of((me ^ flipped(p, n)) * mine, mine)
        source = own_ref if p < n // 2 else other_ref
        q = p % (n // 2)
        fac_ref[pl.ds(to, mine), :] = source[q * mine : (q + 1) * mine, :]
    row = lax.broadcasted_iota(jnp.int32, (16, scen), 0)
    column = lax.broadcasted_iota(jnp.int32, (16, scen), 1)
    tail = jnp.where(tail_ref[...] == 1, 1.0, 0.0)
    at_var = jnp.where(column == var_ref[0], 1.0, 0.0)
    marked = jnp.where(row == 0, tail, jnp.where(row == 1, at_var, 0.0)).astype(jnp.bfloat16)
    marked = jnp.concatenate([marked, marked], axis=1)
    acc_ref[...] = jnp.zeros_like(acc_ref)
    slots = load_ref.shape[1] // BLK

    def block(b, carry):
        at = pl.ds(pl.multiple_of(b * BLK, BLK), BLK)
        chosen = [fac_ref[:, pl.ds(pl.multiple_of(pat_ref[b, j] * BLK, BLK), BLK)] for j in range(slots)]
        score = lax.dot_general(
            jnp.concatenate(chosen, axis=1), load_ref[at, :], NT, preferred_element_type=jnp.float32
        )
        u = par_ref[0:1, at] + par_ref[1:2, at] * score
        expo = par_ref[2:3, at]
        d = jnp.abs(u) + SHIFT
        t = pl.reciprocal(d, approx=True)
        t = t * (2.0 - d * t)
        h = jnp.full_like(t, Q[-1])
        for q in Q[-2::-1]:
            h = h * t + q
        small = h * (t * jnp.exp2(-(u * u))) * expo
        lost = jnp.where(u > 0.0, small, expo - small)
        high = lost.astype(jnp.bfloat16)
        low = (lost - high.astype(jnp.float32)).astype(jnp.bfloat16)
        place = where_ref[:, at]
        acc_ref[...] += lax.dot_general(
            jnp.concatenate([high, low], axis=1),
            jnp.concatenate([place, place], axis=1),
            NT,
            preferred_element_type=jnp.float32,
        )
        picked = jnp.dot(marked, jnp.concatenate([high, low], axis=0), preferred_element_type=jnp.float32)
        con_ref[:, at] = picked[0:1, :] * (16.0 / scen)
        varc_ref[:, at] = picked[1:2, :]
        return carry

    lax.fori_loop(0, load_ref.shape[0] // BLK, block, 0, unroll=2)
    groups = BLK // R
    lane = lax.broadcasted_iota(jnp.int32, (scen, BLK), 1) // R
    kept = jnp.where(lane == lax.broadcasted_iota(jnp.int32, (scen, BLK), 0) % groups, acc_ref[...], 0.0)
    loss_ref[...] = jnp.sum(kept.reshape(scen // groups, groups, BLK), axis=1).reshape(loss_ref.shape)


def losses(n, pattern, var_index, own, other, loadings, params, where, tail_mask):
    rows = loadings.shape[0]
    scen = 2 * own.shape[0]
    vmem = pl.BlockSpec(memory_space=pltpu.VMEM)
    smem = pl.BlockSpec(memory_space=pltpu.SMEM)
    return pl.pallas_call(
        functools.partial(losses_kernel, n),
        out_shape=(
            jax.ShapeDtypeStruct((n, scen // n * R // BLK, BLK), jnp.float32),
            jax.ShapeDtypeStruct((1, rows), jnp.float32),
            jax.ShapeDtypeStruct((1, rows), jnp.float32),
        ),
        in_specs=[smem, smem] + [vmem] * 6,
        out_specs=(vmem, vmem, vmem),
        scratch_shapes=[
            pltpu.VMEM((scen, own.shape[1]), jnp.bfloat16),
            pltpu.VMEM((scen, BLK), jnp.float32),
        ],
        compiler_params=pltpu.CompilerParams(vmem_limit_bytes=24 << 20),
        cost_estimate=pl.CostEstimate(
            flops=2 * rows * scen * 512, bytes_accessed=rows * 1024, transcendentals=2 * rows * scen
        ),
        name="losses",
    )(pattern, var_index, own, other, loadings, params, where, tail_mask[None])


def finish_kernel(factor, parts_ref, out_ref):
    mine = out_ref.shape[1]
    groups = BLK // R
    total = jnp.sum(parts_ref[...], axis=0)
    rows = jnp.concatenate(
        [jnp.broadcast_to(total[k : k + 1, :], (groups, BLK)) for k in range(total.shape[0])], axis=0
    )
    lane = lax.broadcasted_iota(jnp.int32, (mine, BLK), 1)
    kept = jnp.where(lane // R == lax.broadcasted_iota(jnp.int32, (mine, BLK), 0) % groups, rows, 0.0)
    lane = lax.broadcasted_iota(jnp.int32, (R, BLK), 1)
    spread = (lane % R == lax.broadcasted_iota(jnp.int32, (R, BLK), 0)).astype(jnp.float32)
    out_ref[...] = factor * lax.dot_general(
        spread, kept, NT, precision=lax.Precision.HIGHEST, preferred_element_type=jnp.float32
    )


def finish(parts, mine, factor):
    return pl.pallas_call(
        functools.partial(finish_kernel, factor),
        out_shape=jax.ShapeDtypeStruct((R, mine), jnp.float32),
        name="finish",
    )(parts)


def local(factors, loadings, pattern, threshold, rho, exposure, region, tail_mask, var_index):
    n = lax.axis_size("scen")
    mine = factors.shape[0]
    rows = loadings.shape[0]

    def swapped(x, step):
        return lax.ppermute(x, "scen", [(i, i ^ step) for i in range(n)])

    params, where = prepare(loadings, threshold, rho, exposure, region)
    held = factors
    step = n // 2
    while step > 1:
        held = jnp.concatenate([held, swapped(held, step)], axis=0)
        step //= 2
    other = swapped(held, 1)
    loss, con, varc = losses(n, pattern, var_index, held, other, loadings, params, where, tail_mask)
    parts = lax.all_to_all(loss, "scen", 0, 0)
    own_loss = finish(parts, mine, R / (rows * n))
    return own_loss, con.reshape(rows), varc.reshape(rows)


def solution(mesh):
    split = ("groups", "scen")
    return jax.shard_map(
        local,
        mesh=mesh,
        in_specs=(
            P(split, None),
            P(split, None),
            P(split, None),
            P(split),
            P(split),
            P(split),
            P(split),
            P("groups"),
            P("groups"),
        ),
        out_specs=(P(None, split), P(split), P(split)),
        check_vma=False,
    )
```

time: 121 us -> 48.2 us (0.40)
  blocking collectives: 82.6 us -> 12.7 us
  matrix products: 12.9 us -> 0 us
  Pallas kernels: 0 us -> 10.9 us
  local copies, waits for them, and re-layouts: 16.3 us -> 5.92 us
  waiting for transfers between devices: 0 us -> 7.64 us
  starting transfers between devices: 0 us -> 7.52 us
  other arithmetic: 7.81 us -> 1.53 us
    psum x1 -> x0, blocking collectives: 57.8 us -> none  [local(): summed = lax.psum(losses, 'scen')]
    all_gather x1 -> x0, blocking collectives: 24.8 us -> none  [local(): lax.all_gather(factors, 'scen', axis=0, tiled=True)]
    dot_general x6 -> x0, matrix products: 12.9 us -> none  [the longest x4 10.9 us: slot_scores(): jnp.einsum('bok,pbk->bop', loading_block_list[:, :, opening_position, :],...]
    all_to_all x0 -> x1, blocking collectives: none -> 12.7 us  [local(): parts = lax.all_to_all(loss, 'scen', 0, 0)]
    pallas_call x0 -> x3, Pallas kernels: none -> 10.9 us  [the longest x1 8.75 us: losses(): pl.pallas_call(functools.partial(losses_kernel, n), out_shape=(jax.ShapeD...]
    ppermute x0 -> x4, waiting for transfers between devices: none -> 7.64 us  [swapped(): return lax.ppermute(x, 'scen', [(i, i ^ step) for i in range(n)])]
    ppermute x0 -> x4, starting transfers between devices: none -> 7.52 us  [swapped(): return lax.ppermute(x, 'scen', [(i, i ^ step) for i in range(n)])]
    gather x4 -> x0, local copies, waits for them, and re-layouts: 6.71 us -> none  [slot_scores(): chosen = jnp.take(pieces, pattern[:, opening_position], axis=1)]
  transfers between devices with their start and end apart: 0 -> 4, of which waited for: 0 -> 3; matrix products, arithmetic and copies ran while one was open for 0% -> 3% of each run, Pallas kernels for 0% -> 2%
where the time goes in v1:
time: 48.2 us; the launch traced here: 47.5 us
  blocking collectives  12.7 us (26%)
  Pallas kernels  10.9 us (23%)
  waiting for transfers between devices  7.64 us (16%)
  starting transfers between devices  7.52 us (16%)
  local copies, waits for them, and re-layouts  5.92 us (12%)
  other arithmetic  1.53 us (3%)
  between operations  1.34 us (3%)
    all_to_all x1, blocking collectives, local(): parts = lax.all_to_all(loss, 'scen', 0, 0)  12.7 us
    pallas_call x1, Pallas kernels, losses(): pl.pallas_call(functools.partial(losses_kernel, n), out_shape=(jax.ShapeD...  8.75 us
    ppermute x4, waiting for transfers between devices, swapped(): return lax.ppermute(x, 'scen', [(i, i ^ step) for i in range(n)])  7.64 us
    ppermute x4, starting transfers between devices, swapped(): return lax.ppermute(x, 'scen', [(i, i ^ step) for i in range(n)])  7.52 us
    unnamed x16, local copies, waits for them, and re-layouts  5.91 us
    concatenate x2, other arithmetic, local(): held = jnp.concatenate([held, swapped(held, step)], axis=0)  1.53 us
    pallas_call x1, Pallas kernels, finish(): pl.pallas_call(functools.partial(finish_kernel, factor), out_shape=jax.Sh...  1.46 us
  transfers between devices with their start and end apart: 4, of which 3 were waited for; matrix products, arithmetic and copies ran while one was open for 3% of the time, Pallas kernels for 2%

profile of v1, /device:TPU:0, one launch (start us, length us, event | category | flops | bytes accessed | tf_op | source)
XLA Modules:
  0.0 47.5 jit_solution(8884142302773706064)
XLA Ops:
  0.6 0.0 copy-start.5
  0.6 4.1 %collective-permute-start = (bf16[16,1024]{1,0:T(8,128)(2,1)}, bf16[16,1024]{1,0:T(8,128)(2,1)S(1)}, u32[]{:S(2)}, u32[]{:S(2)}) collective-permute-start(bf16[16,1024]{1,0:T(8,128)(2,1)} %param.9), channel_id=1, source_target_pairs={{0,8},{1,9},{2,10},{3,11},{4,12},{5,13},{6,14},{7,15},{8,0},{9,1},... | collective-permute-start | bytes 98312 | tf_op jit(solution)/shard_map/ppermute | solution.py:186
  4.7 2.5 %collective-permute-done = bf16[16,1024]{1,0:T(8,128)(2,1)S(1)} collective-permute-done((bf16[16,1024]{1,0:T(8,128)(2,1)}, bf16[16,1024]{1,0:T(8,128)(2,1)S(1)}, u32[]{:S(2)}, u32[]{:S(2)}) %collective-permute-start) | collective-permute-done | bytes 32800 | tf_op jit(solution)/shard_map/ppermute | solution.py:186
  7.2 0.8 %pad_maximum_fusion.1 = bf16[32,1024]{1,0:T(8,128)(2,1)S(1)} fusion(bf16[16,1024]{1,0:T(8,128)(2,1)S(1)} %collective-permute-done, bf16[16,1024]{1,0:T(8,128)(2,1)} %param.9), kind=kLoop, calls=%fused_computation.1 | loop fusion | flops 131072 | bytes 131072 | tf_op jit(solution)/shard_map/concatenate | solution.py:192
  8.0 1.6 %collective-permute-start.1 = (bf16[32,1024]{1,0:T(8,128)(2,1)S(1)}, bf16[32,1024]{1,0:T(8,128)(2,1)S(1)}, u32[]{:S(2)}, u32[]{:S(2)}) collective-permute-start(bf16[32,1024]{1,0:T(8,128)(2,1)S(1)} %pad_maximum_fusion.1), channel_id=1, source_target_pairs={{0,4},{1,5},{2,6},{3,7},{4,0},{5,1},{6,2},{7,3},{8,12},{9,13},{10,... | collective-permute-start | bytes 196616 | tf_op jit(solution)/shard_map/ppermute | solution.py:186
  9.5 0.8 %constant_dynamic-update-slice_fusion.3 = bf16[128,1024]{1,0:T(8,128)(2,1)S(1)} fusion(bf16[16,1024]{1,0:T(8,128)(2,1)} %param.9), kind=kLoop, calls=%fused_computation.5 | loop fusion | bytes 65536
  10.3 2.0 %collective-permute-done.1 = bf16[32,1024]{1,0:T(8,128)(2,1)S(1)} collective-permute-done((bf16[32,1024]{1,0:T(8,128)(2,1)S(1)}, bf16[32,1024]{1,0:T(8,128)(2,1)S(1)}, u32[]{:S(2)}, u32[]{:S(2)}) %collective-permute-start.1) | collective-permute-done | bytes 65568 | tf_op jit(solution)/shard_map/ppermute | solution.py:186
  12.2 0.8 %pad_maximum_fusion = bf16[64,1024]{1,0:T(8,128)(2,1)S(1)} fusion(bf16[32,1024]{1,0:T(8,128)(2,1)S(1)} %collective-permute-done.1, bf16[16,1024]{1,0:T(8,128)(2,1)S(1)} %collective-permute-done, bf16[16,1024]{1,0:T(8,128)(2,1)} %param.9), kind=kLoop, calls=%fused_computation | loop fusion | flops 393216 | bytes 262144 | tf_op jit(solution)/shard_map/concatenate | solution.py:192
  13.0 1.8 %collective-permute-start.2 = (bf16[64,1024]{1,0:T(8,128)(2,1)S(1)}, bf16[64,1024]{1,0:T(8,128)(2,1)S(1)}, u32[]{:S(2)}, u32[]{:S(2)}) collective-permute-start(bf16[64,1024]{1,0:T(8,128)(2,1)S(1)} %pad_maximum_fusion), channel_id=1, source_target_pairs={{0,2},{1,3},{2,0},{3,1},{4,6},{5,7},{6,4},{7,5},{8,10},{9,11},{10,... | collective-permute-start | bytes 393224 | tf_op jit(solution)/shard_map/ppermute | solution.py:186
  14.8 3.2 %collective-permute-done.2 = bf16[64,1024]{1,0:T(8,128)(2,1)S(1)} collective-permute-done((bf16[64,1024]{1,0:T(8,128)(2,1)S(1)}, bf16[64,1024]{1,0:T(8,128)(2,1)S(1)}, u32[]{:S(2)}, u32[]{:S(2)}) %collective-permute-start.2) | collective-permute-done | bytes 131104 | tf_op jit(solution)/shard_map/ppermute | solution.py:186
  18.0 0.1 collective-permute-start.3
  18.8 0.8 %copy.12.pat_ref = s32[16,4]{1,0:T(8,128)S(1)} copy(s32[16,4]{0,1:T(4,128)} %param.11) | data formatting | bytes 512 | tf_op args[2]
  19.5 0.0 copy-start
  19.5 1.6 %copy-done = bf16[2048,512]{1,0:T(8,128)(2,1)S(1)} copy-done((bf16[2048,512]{1,0:T(8,128)(2,1)S(1)}, bf16[2048,512]{1,0:T(8,128)(2,1)}, u32[]{:S(2)}) %copy-start) | copy-done | bytes 2097176
  21.1 0.0 copy-start.1
  21.1 0.7 %copy-done.1 = f32[2048]{0:T(1024)S(1)} copy-done((f32[2048]{0:T(1024)S(1)}, f32[2048]{0:T(1024)}, u32[]{:S(2)}) %copy-start.1) | copy-done | bytes 8216
  21.8 0.0 copy-start.2
  21.8 0.7 %copy-done.2 = f32[2048]{0:T(1024)S(1)} copy-done((f32[2048]{0:T(1024)S(1)}, f32[2048]{0:T(1024)}, u32[]{:S(2)}) %copy-start.2) | copy-done | bytes 8216
  22.5 0.0 copy-start.3
  22.5 0.7 %copy-done.3 = f32[2048]{0:T(1024)S(1)} copy-done((f32[2048]{0:T(1024)S(1)}, f32[2048]{0:T(1024)}, u32[]{:S(2)}) %copy-start.3) | copy-done | bytes 8216
  23.2 0.0 copy-start.4
  23.2 0.7 %copy-done.4 = s32[2048]{0:T(1024)S(1)} copy-done((s32[2048]{0:T(1024)S(1)}, s32[2048]{0:T(1024)}, u32[]{:S(2)}) %copy-start.4) | copy-done | bytes 8216
  23.9 0.7 %prepare.1 = (f32[8,2048]{1,0:T(8,128)S(1)}, bf16[128,2048]{1,0:T(8,128)(2,1)S(1)}) custom-call(bf16[2048,512]{1,0:T(8,128)(2,1)S(1)} %copy-done, f32[1,2048]{1,0:T(1,128)S(1)} %bitcast.7, f32[1,2048]{1,0:T(1,128)S(1)} %bitcast.8, f32[1,2048]{1,0:T(1,128)S(1)} %bitcast.9, s32[1,2048]{1,0:T(1,128)S(1)} %bitcast.10), custom_call_target="tpu_custom_call" | custom-call | flops 268435456 | bytes 3145728 | tf_op jit(solution)/shard_map/prepare/pallas_call | solution.py:60
  24.7 0.0 collective-permute-done.3.other_ref
  24.7 0.0 copy-done.5
  24.7 8.8 %losses.1 = (f32[16,2,128]{2,1,0:T(2,128)S(1)}, f32[1,2048]{1,0:T(1,128)}, f32[1,2048]{1,0:T(1,128)}) custom-call(s32[16,4]{1,0:T(8,128)S(1)} %copy.12.pat_ref, s32[1]{0:T(128)S(6)} %copy.16.var_ref, bf16[128,1024]{1,0:T(8,128)(2,1)S(1)} %constant_dynamic-update-slice_fusion.own_ref, bf16[128,1024]{1,0:T(8,128)(2,1)S(1)} %collective-permute-done.3.other_ref, ...), custom_call_target="tpu_custom_call" | custom-call | flops 536870912 | bytes 2097152 | tf_op jit(solution)/shard_map/losses/pallas_call | solution.py:135
  33.4 12.7 %all_to_all.5.parts_ref = f32[16,2,128]{2,1,0:T(2,128)} all-to-all(f32[16,2,128]{2,1,0:T(2,128)S(1)} %get-tuple-element.10), channel_id=1, replica_groups=mesh['groups'=2,'scen'=16] {'scen'}, dimensions={0} | all-to-all | bytes 32768 | tf_op jit(solution)/shard_map/all_to_all | solution.py:196
  46.1 1.5 %finish.1 = f32[16,16]{1,0:T(8,128)} custom-call(f32[16,2,128]{2,1,0:T(2,128)} %all_to_all.5.parts_ref), custom_call_target="tpu_custom_call" | custom-call | tf_op jit(solution)/shard_map/finish/pallas_call | solution.py:173
  (3 shorter events, 0.0 us)
Async XLA Ops:
  0.6 24.0 %copy-start.5 = (s32[256]{0:T(256)S(1)}, s32[256]{0:T(256)}, u32[]{:S(2)}) copy-start(s32[256]{0:T(256)} %param.16) | copy-start | bytes 3076
  0.6 6.6 %collective-permute-start = (bf16[16,1024]{1,0:T(8,128)(2,1)}, bf16[16,1024]{1,0:T(8,128)(2,1)S(1)}, u32[]{:S(2)}, u32[]{:S(2)}) collective-permute-start(bf16[16,1024]{1,0:T(8,128)(2,1)} %param.9), channel_id=1, source_target_pairs={{0,8},{1,9},{2,10},{3,11},{4,12},{5,13},{6,14},{7,15},{8,0},{9,1},... | collective-permute-start | bytes 98312 | tf_op jit(solution)/shard_map/ppermute | solution.py:186
  8.0 4.3 %collective-permute-start.1 = (bf16[32,1024]{1,0:T(8,128)(2,1)S(1)}, bf16[32,1024]{1,0:T(8,128)(2,1)S(1)}, u32[]{:S(2)}, u32[]{:S(2)}) collective-permute-start(bf16[32,1024]{1,0:T(8,128)(2,1)S(1)} %pad_maximum_fusion.1), channel_id=1, source_target_pairs={{0,4},{1,5},{2,6},{3,7},{4,0},{5,1},{6,2},{7,3},{8,12},{9,13},{10,... | collective-permute-start | bytes 196616 | tf_op jit(solution)/shard_map/ppermute | solution.py:186
  13.0 5.0 %collective-permute-start.2 = (bf16[64,1024]{1,0:T(8,128)(2,1)S(1)}, bf16[64,1024]{1,0:T(8,128)(2,1)S(1)}, u32[]{:S(2)}, u32[]{:S(2)}) collective-permute-start(bf16[64,1024]{1,0:T(8,128)(2,1)S(1)} %pad_maximum_fusion), channel_id=1, source_target_pairs={{0,2},{1,3},{2,0},{3,1},{4,6},{5,7},{6,4},{7,5},{8,10},{9,11},{10,... | collective-permute-start | bytes 393224 | tf_op jit(solution)/shard_map/ppermute | solution.py:186
  18.0 6.6 %collective-permute-start.3 = (bf16[128,1024]{1,0:T(8,128)(2,1)S(1)}, bf16[128,1024]{1,0:T(8,128)(2,1)S(1)}, u32[]{:S(2)}, u32[]{:S(2)}) collective-permute-start(bf16[128,1024]{1,0:T(8,128)(2,1)S(1)} %constant_dynamic-update-slice_fusion.own_ref), channel_id=1, source_target_pairs={{0,1},{1,0},{2,3},{3,2},{4,5},{5,4},{6,7},{7,6},{8,9},{9,8},{10,11... | collective-permute-start | bytes 786440 | tf_op jit(solution)/shard_map/ppermute | solution.py:186
  19.5 1.6 %copy-start = (bf16[2048,512]{1,0:T(8,128)(2,1)S(1)}, bf16[2048,512]{1,0:T(8,128)(2,1)}, u32[]{:S(2)}) copy-start(bf16[2048,512]{1,0:T(8,128)(2,1)} %load_ref.3) | copy-start | bytes 6291460
  21.1 0.7 %copy-start.1 = (f32[2048]{0:T(1024)S(1)}, f32[2048]{0:T(1024)}, u32[]{:S(2)}) copy-start(f32[2048]{0:T(1024)} %param.12) | copy-start | bytes 24580
  21.8 0.7 %copy-start.2 = (f32[2048]{0:T(1024)S(1)}, f32[2048]{0:T(1024)}, u32[]{:S(2)}) copy-start(f32[2048]{0:T(1024)} %param.13) | copy-start | bytes 24580
  22.5 0.7 %copy-start.3 = (f32[2048]{0:T(1024)S(1)}, f32[2048]{0:T(1024)}, u32[]{:S(2)}) copy-start(f32[2048]{0:T(1024)} %param.14) | copy-start | bytes 24580
  23.2 0.7 %copy-start.4 = (s32[2048]{0:T(1024)S(1)}, s32[2048]{0:T(1024)}, u32[]{:S(2)}) copy-start(s32[2048]{0:T(1024)} %param.15) | copy-start | bytes 24580

commit v2 on v1

v2 whole, which is shorter than its diff:
```python
import functools
import math

import jax
import jax.numpy as jnp
from jax import lax
from jax.experimental import pallas as pl
from jax.experimental.pallas import tpu as pltpu
from jax.sharding import PartitionSpec as P

R = 16
BLK = 128
GROUPS = BLK // R
STRIP = 64
NT = (((1,), (1,)), ((), ()))
LOG2E = math.log2(math.e)
FAR = 2.0
SHIFT = 1.7 / math.sqrt(LOG2E)
Q = tuple(
    c / math.sqrt(LOG2E) ** (i + 1)
    for i, c in enumerate(
        (0.3388296961784363, 0.5761929750442505, 0.7263157367706299, 0.5614434480667114, -1.9068398475646973)
    )
)


def flipped(p, n):
    out = 0
    step = 1
    while step < n:
        out = 2 * out + (p & 1)
        p //= 2
        step *= 2
    return out


def prepare_kernel(
    var_ref, load_hbm, thr_hbm, rho_hbm, expo_hbm, region_hbm, tail_hbm, par_ref, where_ref, mark_ref,
    load_ref, thr_ref, rho_ref, expo_ref, region_ref, tail_ref, sems,
):
    rows, width = load_ref.shape
    pairs = (
        (thr_hbm, thr_ref), (rho_hbm, rho_ref), (expo_hbm, expo_ref), (region_hbm, region_ref), (tail_hbm, tail_ref),
    )
    copies = [pltpu.make_async_copy(a, b, sems.at[i]) for i, (a, b) in enumerate(pairs)]
    parts = 4
    piece = rows // parts
    for i in range(parts):
        at = pl.ds(i * piece, piece)
        copies.append(pltpu.make_async_copy(load_hbm.at[at, :], load_ref.at[at, :], sems.at[len(pairs) + i]))
    for copy in copies:
        copy.start()
    for copy in copies[: len(pairs)]:
        copy.wait()
    scen = tail_ref.shape[1]
    diagonal = lax.broadcasted_iota(jnp.int32, (BLK, BLK), 0) == lax.broadcasted_iota(jnp.int32, (BLK, BLK), 1)
    for c in range(scen // BLK):
        at = slice(c * BLK, (c + 1) * BLK)
        tail = jnp.where(tail_ref[:, at] == 1, 1.0, 0.0)
        mark_ref[0, at, :] = jnp.broadcast_to(tail, (BLK, BLK)).T
        scenario = lax.broadcasted_iota(jnp.int32, (BLK, BLK), 0) + c * BLK
        mark_ref[1, at, :] = jnp.where(scenario == var_ref[0:1, :], 1.0, 0.0)
    row_region = lax.broadcasted_iota(jnp.int32, (BLK, rows), 0) % R
    where_ref[...] = jnp.where(row_region == region_ref[...], 1.0, 0.0).astype(jnp.bfloat16)
    par_ref[...] = jnp.zeros_like(par_ref)
    for i in range(parts):
        copies[len(pairs) + i].wait()
        for b in range(i * piece // BLK, (i + 1) * piece // BLK):
            at = slice(b * BLK, (b + 1) * BLK)
            block = load_ref[at, :]
            gram = lax.dot_general(block, block, NT, preferred_element_type=jnp.float32)
            mean_sq = jnp.sum(jnp.where(diagonal, gram, 0.0), axis=0, keepdims=True) * (1.0 / width)
            rho = rho_ref[:, at]
            scale = jnp.sqrt(rho / (width * (mean_sq + 1e-06)))
            to_z = math.sqrt(0.5) / jnp.sqrt(1.0 - rho)
            par_ref[0:1, at] = -thr_ref[:, at] * to_z
            par_ref[1:2, at] = scale * to_z
            par_ref[2:3, at] = expo_ref[:, at]


def prepare(loadings, threshold, rho, exposure, region, tail_mask, var_index):
    rows = loadings.shape[0]
    scen = tail_mask.shape[0]
    hbm = pl.BlockSpec(memory_space=pltpu.HBM)
    return pl.pallas_call(
        prepare_kernel,
        out_shape=(
            jax.ShapeDtypeStruct((8, rows), jnp.float32),
            jax.ShapeDtypeStruct((BLK, rows), jnp.bfloat16),
            jax.ShapeDtypeStruct((2, scen, BLK), jnp.float32),
        ),
        in_specs=[pl.BlockSpec(memory_space=pltpu.VMEM)] + [hbm] * 6,
        scratch_shapes=[
            pltpu.VMEM(loadings.shape, loadings.dtype),
            pltpu.VMEM((1, rows), jnp.float32),
            pltpu.VMEM((1, rows), jnp.float32),
            pltpu.VMEM((1, rows), jnp.float32),
            pltpu.VMEM((1, rows), jnp.int32),
            pltpu.VMEM((1, scen), jnp.int32),
            pltpu.SemaphoreType.DMA((9,)),
        ],
        compiler_params=pltpu.CompilerParams(vmem_limit_bytes=16 << 20),
        cost_estimate=pl.CostEstimate(
            flops=2 * rows * BLK * loadings.shape[1], bytes_accessed=3 * rows * 512, transcendentals=2 * rows
        ),
        name="prepare",
    )(
        jnp.broadcast_to(var_index[None], (8, BLK)),
        *(
            pltpu.with_memory_space_constraint(x, pltpu.HBM)
            for x in (loadings, threshold[None], rho[None], exposure[None], region[None], tail_mask[None])
        ),
    )


def losses_kernel(
    n, pat_hbm, own_ref, other_ref, load_ref, par_ref, where_ref, mark_ref, loss_ref, con_ref, varc_ref,
    pat_ref, fac_ref, score_ref, lost_ref, sem,
):
    fetch = pltpu.make_async_copy(pat_hbm, pat_ref, sem)
    fetch.start()
    me = lax.axis_index("scen")
    scen = fac_ref.shape[0]
    mine = scen // n
    for p in range(n):
        to = pl.multiple_of((me ^ flipped(p, n)) * mine, mine)
        source = own_ref if p < n // 2 else other_ref
        q = p % (n // 2)
        fac_ref[pl.ds(to, mine), :] = source[q * mine : (q + 1) * mine, :]
    fetch.wait()
    rows, width = load_ref.shape
    blocks = rows // BLK
    slots = score_ref.shape[0]

    def score(b):
        chosen = [fac_ref[:, pl.ds(pl.multiple_of(pat_ref[j, b] * BLK, BLK), BLK)] for j in range(width // BLK)]
        score_ref[b % slots] = lax.dot_general(
            jnp.concatenate(chosen, axis=1),
            load_ref[b * BLK : (b + 1) * BLK, :],
            NT,
            preferred_element_type=jnp.float32,
        )

    def weigh(b):
        at = slice(b * BLK, (b + 1) * BLK)
        shift = par_ref[0:1, at]
        scale = par_ref[1:2, at]
        expo = par_ref[2:3, at]
        half = 0.5 * expo
        tails = jnp.zeros((8, BLK), jnp.float32)
        vars_ = jnp.zeros((8, BLK), jnp.float32)
        for c in range(0, scen, STRIP):
            strip = slice(c, c + STRIP)
            z = shift + scale * score_ref[b % slots, strip, :]
            t = pl.reciprocal(z + SHIFT, approx=True)
            h = jnp.full_like(t, Q[-1])
            for q in Q[-2::-1]:
                h = h * t + q
            far = (h * t) * (jnp.exp2((z * z) * -LOG2E) * expo)
            lost = jnp.where(z > FAR, far, half - half * lax.erf(z))
            high = lost.astype(jnp.bfloat16)
            lost_ref[b % slots, strip, 0:BLK] = high
            lost_ref[b % slots, strip, BLK:] = (lost - high.astype(jnp.float32)).astype(jnp.bfloat16)
            tails += jnp.sum((lost * mark_ref[0, strip, :]).reshape(STRIP // 8, 8, BLK), axis=0)
            vars_ += jnp.sum((lost * mark_ref[1, strip, :]).reshape(STRIP // 8, 8, BLK), axis=0)
        con_ref[b : b + 1, :] = jnp.sum(tails, axis=0, keepdims=True) * (16.0 / scen)
        varc_ref[b : b + 1, :] = jnp.sum(vars_, axis=0, keepdims=True)

    def place(b):
        region = where_ref[:, b * BLK : (b + 1) * BLK]
        return lax.dot_general(
            lost_ref[b % slots], jnp.concatenate([region, region], axis=1), NT, preferred_element_type=jnp.float32
        )

    total = jnp.zeros((scen, BLK), jnp.float32)
    for b in range(blocks + 2):
        if b < blocks:
            score(b)
        if 1 <= b <= blocks:
            weigh(b - 1)
        if 2 <= b:
            total += place(b - 2)
    lane = lax.broadcasted_iota(jnp.int32, (scen, BLK), 1) // R
    kept = jnp.where(lane == lax.broadcasted_iota(jnp.int32, (scen, BLK), 0) % GROUPS, total, 0.0)
    loss_ref[...] = jnp.sum(kept.reshape(scen // GROUPS, GROUPS, BLK), axis=1).reshape(loss_ref.shape)


def losses(n, pattern, own, other, loadings, params, where, marks):
    rows = loadings.shape[0]
    scen = 2 * own.shape[0]
    vmem = pl.BlockSpec(memory_space=pltpu.VMEM)
    hbm = pl.BlockSpec(memory_space=pltpu.HBM)
    return pl.pallas_call(
        functools.partial(losses_kernel, n),
        out_shape=(
            jax.ShapeDtypeStruct((n, scen // n // GROUPS, BLK), jnp.float32),
            jax.ShapeDtypeStruct((rows // BLK, BLK), jnp.float32),
            jax.ShapeDtypeStruct((rows // BLK, BLK), jnp.float32),
        ),
        in_specs=[hbm] + [vmem] * 6,
        out_specs=(vmem, vmem, vmem),
        scratch_shapes=[
            pltpu.SMEM((pattern.shape[1], pattern.shape[0]), jnp.int32),
            pltpu.VMEM((scen, own.shape[1]), jnp.bfloat16),
            pltpu.VMEM((3, scen, BLK), jnp.float32),
            pltpu.VMEM((3, scen, 2 * BLK), jnp.bfloat16),
            pltpu.SemaphoreType.DMA,
        ],
        compiler_params=pltpu.CompilerParams(vmem_limit_bytes=24 << 20),
        cost_estimate=pl.CostEstimate(
            flops=2 * rows * scen * 512, bytes_accessed=rows * 1024, transcendentals=3 * rows * scen
        ),
        name="losses",
    )(pltpu.with_memory_space_constraint(pattern.T, pltpu.HBM), own, other, loadings, params, where, marks)


def finish_kernel(factor, parts_ref, out_ref):
    mine = out_ref.shape[1]
    total = jnp.sum(parts_ref[...], axis=0) * factor
    rows = jnp.concatenate(
        [jnp.broadcast_to(total[k : k + 1, :], (GROUPS, BLK)) for k in range(total.shape[0])], axis=0
    )
    lane = lax.broadcasted_iota(jnp.int32, (mine, BLK), 1)
    kept = jnp.where(lane // R == lax.broadcasted_iota(jnp.int32, (mine, BLK), 0) % GROUPS, rows, 0.0)
    lane = lax.broadcasted_iota(jnp.int32, (R, BLK), 1)
    spread = (lane % R == lax.broadcasted_iota(jnp.int32, (R, BLK), 0)).astype(jnp.float32)
    out_ref[...] = lax.dot_general(
        spread, kept, NT, precision=lax.Precision.HIGHEST, preferred_element_type=jnp.float32
    )


def finish(parts, mine, factor):
    return pl.pallas_call(
        functools.partial(finish_kernel, factor),
        out_shape=jax.ShapeDtypeStruct((R, mine), jnp.float32),
        name="finish",
    )(parts)


def local(factors, loadings, pattern, threshold, rho, exposure, region, tail_mask, var_index):
    n = lax.axis_size("scen")
    mine = factors.shape[0]
    rows = loadings.shape[0]

    def swapped(x, step):
        return lax.ppermute(x, "scen", [(i, i ^ step) for i in range(n)])

    step = n // 2
    prepared = prepare(loadings, threshold, rho, exposure, region, tail_mask, var_index)
    far, prepared = lax.optimization_barrier((swapped(factors, step), prepared))
    held = jnp.concatenate([factors, far], axis=0)
    step //= 2
    while step > 1:
        held = jnp.concatenate([held, swapped(held, step)], axis=0)
        step //= 2
    other = swapped(held, 1)
    loss, con, varc = losses(n, pattern, held, other, loadings, *prepared)
    parts = lax.all_to_all(loss, "scen", 0, 0)
    own_loss = finish(parts, mine, R / (rows * n))
    return own_loss, con.reshape(rows), varc.reshape(rows)


def solution(mesh):
    split = ("groups", "scen")
    return jax.shard_map(
        local,
        mesh=mesh,
        in_specs=(
            P(split, None),
            P(split, None),
            P(split, None),
            P(split),
            P(split),
            P(split),
            P(split),
            P("groups"),
            P("groups"),
        ),
        out_specs=(P(None, split), P(split), P(split)),
        check_vma=False,
    )
```

time: 48.2 us -> 37.1 us (0.77)
  local copies, waits for them, and re-layouts: 5.92 us -> 0.03 us
  Pallas kernels: 10.9 us -> 8.45 us
  other arithmetic: 1.53 us -> 0.02 us
  blocking collectives: 12.7 us -> 11.8 us
    unnamed x16 -> x7, local copies, waits for them, and re-layouts: 5.91 us -> 0.02 us
    pallas_call x1, Pallas kernels: 8.75 us -> 4.46 us  [losses(): pl.pallas_call(functools.partial(losses_kernel, n), out_shape=(jax.ShapeD...]
    pallas_call x1, Pallas kernels: 0.73 us -> 2.52 us  [prepare(): pl.pallas_call(prepare_kernel, out_shape=(jax.ShapeDtypeStruct((8, rows),...]
    concatenate x2 -> x1, other arithmetic: 1.53 us -> 0.01 us  [local(): held = jnp.concatenate([held, swapped(held, step)], axis=0)]
    all_to_all x1, blocking collectives: 12.7 us -> 11.8 us  [local(): parts = lax.all_to_all(loss, 'scen', 0, 0)]
  transfers between devices with their start and end apart: 4 -> 4, of which waited for: 3 -> 3; matrix products, arithmetic and copies ran while one was open for 3% -> 0% of each run, Pallas kernels for 2% -> 7%
where the time goes in v2:
time: 37.1 us; the launch traced here: 36.7 us
  blocking collectives  11.8 us (32%)
  Pallas kernels  8.45 us (23%)
  waiting for transfers between devices  7.65 us (21%)
  starting transfers between devices  7.4 us (20%)
  between operations  1.37 us (4%)
    all_to_all x1, blocking collectives, local(): parts = lax.all_to_all(loss, 'scen', 0, 0)  11.8 us
    ppermute x4, waiting for transfers between devices, swapped(): return lax.ppermute(x, 'scen', [(i, i ^ step) for i in range(n)])  7.65 us
    ppermute x4, starting transfers between devices, swapped(): return lax.ppermute(x, 'scen', [(i, i ^ step) for i in range(n)])  7.4 us
    pallas_call x1, Pallas kernels, losses(): pl.pallas_call(functools.partial(losses_kernel, n), out_shape=(jax.ShapeD...  4.46 us
    pallas_call x1, Pallas kernels, prepare(): pl.pallas_call(prepare_kernel, out_shape=(jax.ShapeDtypeStruct((8, rows),...  2.52 us
    pallas_call x1, Pallas kernels, finish(): pl.pallas_call(functools.partial(finish_kernel, factor), out_shape=jax.Sh...  1.46 us
  transfers between devices with their start and end apart: 4, of which 3 were waited for; matrix products, arithmetic and copies ran while one was open for 0% of the time, Pallas kernels for 7%

profile of v2, /device:TPU:0, one launch (start us, length us, event | category | flops | bytes accessed | tf_op | source)
XLA Modules:
  0.0 36.7 jit_solution(4745801027767489012)
XLA Ops:
  0.6 0.0 copy-start.1
  0.6 0.0 copy-start
  0.7 4.1 %collective-permute-start = (bf16[16,1024]{1,0:T(8,128)(2,1)}, bf16[16,1024]{1,0:T(8,128)(2,1)S(1)}, u32[]{:S(2)}, u32[]{:S(2)}) collective-permute-start(bf16[16,1024]{1,0:T(8,128)(2,1)} %param.9), channel_id=1, source_target_pairs={{0,8},{1,9},{2,10},{3,11},{4,12},{5,13},{6,14},{7,15},{8,0},{9,1},... | collective-permute-start | bytes 98312 | tf_op jit(solution)/shard_map/ppermute | solution.py:246
  5.4 2.5 %prepare.1 = (f32[8,2048]{1,0:T(8,128)S(1)}, bf16[128,2048]{1,0:T(8,128)(2,1)S(1)}, f32[2,256,128]{2,1,0:T(8,128)S(1)}) custom-call(s32[8,128]{1,0:T(8,128)S(1)} %broadcast_in_dim.24.var_ref, bf16[2048,512]{1,0:T(8,128)(2,1)} %load_ref.1, f32[1,2048]{1,0:T(1,128)} %bitcast.10, f32[1,2048]{1,0:T(1,128)} %bitcast.11, f32[1,2048]{1,0:T(1,128)} %bitcast.12, ...), custom_call_target="tpu_custom_call" | custom-call | flops 268435456 | bytes 3145728 | tf_op jit(solution)/shard_map/prepare/pallas_call | solution.py:85
  7.9 0.0 collective-permute-done
  8.0 0.0 copy-done.1
  8.0 1.6 %collective-permute-start.1 = (bf16[32,1024]{1,0:T(8,128)(2,1)S(1)}, bf16[32,1024]{1,0:T(8,128)(2,1)S(1)}, u32[]{:S(2)}, u32[]{:S(2)}) collective-permute-start(bf16[32,1024]{1,0:T(8,128)(2,1)S(1)} %pad_maximum_fusion.1), channel_id=1, source_target_pairs={{0,4},{1,5},{2,6},{3,7},{4,0},{5,1},{6,2},{7,3},{8,12},{9,13},{10,... | collective-permute-start | bytes 196616 | tf_op jit(solution)/shard_map/ppermute | solution.py:246
  9.6 2.7 %collective-permute-done.1 = bf16[32,1024]{1,0:T(8,128)(2,1)S(1)} collective-permute-done((bf16[32,1024]{1,0:T(8,128)(2,1)S(1)}, bf16[32,1024]{1,0:T(8,128)(2,1)S(1)}, u32[]{:S(2)}, u32[]{:S(2)}) %collective-permute-start.1) | collective-permute-done | bytes 65568 | tf_op jit(solution)/shard_map/ppermute | solution.py:246
  12.3 1.6 %collective-permute-start.2 = (bf16[64,1024]{1,0:T(8,128)(2,1)S(1)}, bf16[64,1024]{1,0:T(8,128)(2,1)S(1)}, u32[]{:S(2)}, u32[]{:S(2)}) collective-permute-start(bf16[64,1024]{1,0:T(8,128)(2,1)S(1)} %pad_maximum_fusion), channel_id=1, source_target_pairs={{0,2},{1,3},{2,0},{3,1},{4,6},{5,7},{6,4},{7,5},{8,10},{9,11},{10,... | collective-permute-start | bytes 393224 | tf_op jit(solution)/shard_map/ppermute | solution.py:246
  13.9 3.4 %collective-permute-done.2 = bf16[64,1024]{1,0:T(8,128)(2,1)S(1)} collective-permute-done((bf16[64,1024]{1,0:T(8,128)(2,1)S(1)}, bf16[64,1024]{1,0:T(8,128)(2,1)S(1)}, u32[]{:S(2)}, u32[]{:S(2)}) %collective-permute-start.2) | collective-permute-done | bytes 131104 | tf_op jit(solution)/shard_map/ppermute | solution.py:246
  17.4 0.1 collective-permute-start.3
  17.4 1.5 %collective-permute-done.3.other_ref = bf16[128,1024]{1,0:T(8,128)(2,1)S(1)} collective-permute-done((bf16[128,1024]{1,0:T(8,128)(2,1)S(1)}, bf16[128,1024]{1,0:T(8,128)(2,1)S(1)}, u32[]{:S(2)}, u32[]{:S(2)}) %collective-permute-start.3) | collective-permute-done | bytes 262176 | tf_op jit(solution)/shard_map/ppermute | solution.py:246
  19.0 0.0 copy-done
  19.0 4.5 %losses.1 = (f32[16,2,128]{2,1,0:T(2,128)S(1)}, f32[16,128]{1,0:T(8,128)}, f32[16,128]{1,0:T(8,128)}) custom-call(s32[4,16]{1,0:T(4,128)} %bitcast.14, bf16[128,1024]{1,0:T(8,128)(2,1)S(1)} %constant_dynamic-update-slice_fusion.own_ref, bf16[128,1024]{1,0:T(8,128)(2,1)S(1)} %collective-permute-done.3.other_ref, bf16[2048,512]{1,0:T(8,128)(2,1)S(1)} %copy-done, ...), custom_call_target="tpu_custom_call" | custom-call | flops 536870912 | bytes 2097152 | tf_op jit(solution)/shard_map/losses/pallas_call | solution.py:193
  23.4 11.8 %all_to_all.5.parts_ref = f32[16,2,128]{2,1,0:T(2,128)} all-to-all(f32[16,2,128]{2,1,0:T(2,128)S(1)} %get-tuple-element.20), channel_id=1, replica_groups=mesh['groups'=2,'scen'=16] {'scen'}, dimensions={0} | all-to-all | bytes 32768 | tf_op jit(solution)/shard_map/all_to_all | solution.py:258
  35.3 1.5 %finish.1 = f32[16,16]{1,0:T(8,128)} custom-call(f32[16,2,128]{2,1,0:T(2,128)} %all_to_all.5.parts_ref), custom_call_target="tpu_custom_call" | custom-call | tf_op jit(solution)/shard_map/finish/pallas_call | solution.py:233
  (7 shorter events, 0.0 us)
Async XLA Ops:
  0.6 7.3 %copy-start.1 = (bf16[16,1024]{1,0:T(8,128)(2,1)S(1)}, bf16[16,1024]{1,0:T(8,128)(2,1)}, u32[]{:S(2)}) copy-start(bf16[16,1024]{1,0:T(8,128)(2,1)} %param.9) | copy-start | bytes 98308
  0.6 18.3 %copy-start = (bf16[2048,512]{1,0:T(8,128)(2,1)S(1)}, bf16[2048,512]{1,0:T(8,128)(2,1)}, u32[]{:S(2)}) copy-start(bf16[2048,512]{1,0:T(8,128)(2,1)} %load_ref.1) | copy-start | bytes 6291460
  0.7 7.3 %collective-permute-start = (bf16[16,1024]{1,0:T(8,128)(2,1)}, bf16[16,1024]{1,0:T(8,128)(2,1)S(1)}, u32[]{:S(2)}, u32[]{:S(2)}) collective-permute-start(bf16[16,1024]{1,0:T(8,128)(2,1)} %param.9), channel_id=1, source_target_pairs={{0,8},{1,9},{2,10},{3,11},{4,12},{5,13},{6,14},{7,15},{8,0},{9,1},... | collective-permute-start | bytes 98312 | tf_op jit(solution)/shard_map/ppermute | solution.py:246
  8.0 4.3 %collective-permute-start.1 = (bf16[32,1024]{1,0:T(8,128)(2,1)S(1)}, bf16[32,1024]{1,0:T(8,128)(2,1)S(1)}, u32[]{:S(2)}, u32[]{:S(2)}) collective-permute-start(bf16[32,1024]{1,0:T(8,128)(2,1)S(1)} %pad_maximum_fusion.1), channel_id=1, source_target_pairs={{0,4},{1,5},{2,6},{3,7},{4,0},{5,1},{6,2},{7,3},{8,12},{9,13},{10,... | collective-permute-start | bytes 196616 | tf_op jit(solution)/shard_map/ppermute | solution.py:246
  12.3 5.0 %collective-permute-start.2 = (bf16[64,1024]{1,0:T(8,128)(2,1)S(1)}, bf16[64,1024]{1,0:T(8,128)(2,1)S(1)}, u32[]{:S(2)}, u32[]{:S(2)}) collective-permute-start(bf16[64,1024]{1,0:T(8,128)(2,1)S(1)} %pad_maximum_fusion), channel_id=1, source_target_pairs={{0,2},{1,3},{2,0},{3,1},{4,6},{5,7},{6,4},{7,5},{8,10},{9,11},{10,... | collective-permute-start | bytes 393224 | tf_op jit(solution)/shard_map/ppermute | solution.py:246
  17.4 1.6 %collective-permute-start.3 = (bf16[128,1024]{1,0:T(8,128)(2,1)S(1)}, bf16[128,1024]{1,0:T(8,128)(2,1)S(1)}, u32[]{:S(2)}, u32[]{:S(2)}) collective-permute-start(bf16[128,1024]{1,0:T(8,128)(2,1)S(1)} %constant_dynamic-update-slice_fusion.own_ref), channel_id=1, source_target_pairs={{0,1},{1,0},{2,3},{3,2},{4,5},{5,4},{6,7},{7,6},{8,9},{9,8},{10,11... | collective-permute-start | bytes 786440 | tf_op jit(solution)/shard_map/ppermute | solution.py:246

commit v3 on v2

--- a/solution.py
+++ b/solution.py
@@ -11,7 +11,8 @@
 R = 16
 BLK = 128
 GROUPS = BLK // R
-STRIP = 64
+STRIP = 32
+TOGETHER = 4
 NT = (((1,), (1,)), ((), ()))
 LOG2E = math.log2(math.e)
 FAR = 2.0
@@ -60,7 +61,7 @@
         mark_ref[0, at, :] = jnp.broadcast_to(tail, (BLK, BLK)).T
         scenario = lax.broadcasted_iota(jnp.int32, (BLK, BLK), 0) + c * BLK
         mark_ref[1, at, :] = jnp.where(scenario == var_ref[0:1, :], 1.0, 0.0)
-    row_region = lax.broadcasted_iota(jnp.int32, (BLK, rows), 0) % R
+    row_region = lax.broadcasted_iota(jnp.int32, (R, rows), 0)
     where_ref[...] = jnp.where(row_region == region_ref[...], 1.0, 0.0).astype(jnp.bfloat16)
     par_ref[...] = jnp.zeros_like(par_ref)
     for i in range(parts):
@@ -86,7 +87,7 @@
         prepare_kernel,
         out_shape=(
             jax.ShapeDtypeStruct((8, rows), jnp.float32),
-            jax.ShapeDtypeStruct((BLK, rows), jnp.bfloat16),
+            jax.ShapeDtypeStruct((R, rows), jnp.bfloat16),
             jax.ShapeDtypeStruct((2, scen, BLK), jnp.float32),
         ),
         in_specs=[pl.BlockSpec(memory_space=pltpu.VMEM)] + [hbm] * 6,
@@ -113,43 +114,61 @@
     )
 
 
-def losses_kernel(
-    n, pat_hbm, own_ref, other_ref, load_ref, par_ref, where_ref, mark_ref, loss_ref, con_ref, varc_ref,
-    pat_ref, fac_ref, score_ref, lost_ref, sem,
-):
-    fetch = pltpu.make_async_copy(pat_hbm, pat_ref, sem)
-    fetch.start()
+def turn_kernel(load_ref, turned_ref):
+    for b in range(turned_ref.shape[0]):
+        turned_ref[b] = load_ref[b * BLK : (b + 1) * BLK, :].T
+
+
+def turn(loadings):
+    rows, width = loadings.shape
+    vmem = pl.BlockSpec(memory_space=pltpu.VMEM)
+    return pl.pallas_call(
+        turn_kernel,
+        out_shape=jax.ShapeDtypeStruct((rows // BLK, width, BLK), loadings.dtype),
+        in_specs=[vmem],
+        out_specs=vmem,
+        compiler_params=pltpu.CompilerParams(vmem_limit_bytes=16 << 20),
+        cost_estimate=pl.CostEstimate(flops=0, bytes_accessed=4 * rows * width, transcendentals=0),
+        name="turn",
+    )(loadings)
+
+
+def gathered_from(p, n):
+    return 4 * flipped(p, n // 4)
+
+
+def weigh_kernel(n, last, bits, *refs):
+    pat_ref, load_ref, par_ref, where_ref, mark_ref, con_in, var_in, fac_ref = refs[:8]
+    earlier, refs = refs[8:-6], refs[-6:]
+    loss_ref, con_ref, varc_ref, score_ref, lost_ref, part_ref = refs
     me = lax.axis_index("scen")
-    scen = fac_ref.shape[0]
+    scen = mark_ref.shape[1]
     mine = scen // n
-    for p in range(n):
-        to = pl.multiple_of((me ^ flipped(p, n)) * mine, mine)
-        source = own_ref if p < n // 2 else other_ref
-        q = p % (n // 2)
-        fac_ref[pl.ds(to, mine), :] = source[q * mine : (q + 1) * mine, :]
-    fetch.wait()
-    rows, width = load_ref.shape
-    blocks = rows // BLK
+    here = fac_ref.shape[0]
+    for p in range(here // mine):
+        owner = me ^ (gathered_from(p, n) | bits)
+        part_ref[:, p * mine : (p + 1) * mine, :] = mark_ref[:, pl.ds(pl.multiple_of(owner * mine, mine), mine), :]
+    blocks, width, _ = load_ref.shape
     slots = score_ref.shape[0]
+    batches = lost_ref.shape[0]
 
     def score(b):
         chosen = [fac_ref[:, pl.ds(pl.multiple_of(pat_ref[j, b] * BLK, BLK), BLK)] for j in range(width // BLK)]
-        score_ref[b % slots] = lax.dot_general(
-            jnp.concatenate(chosen, axis=1),
-            load_ref[b * BLK : (b + 1) * BLK, :],
-            NT,
-            preferred_element_type=jnp.float32,
+        score_ref[b % slots] = jnp.dot(
+            jnp.concatenate(chosen, axis=1), load_ref[b], preferred_element_type=jnp.float32
         )
 
     def weigh(b):
         at = slice(b * BLK, (b + 1) * BLK)
+        to = b % TOGETHER * BLK
+        to_low = to + TOGETHER * BLK
         shift = par_ref[0:1, at]
         scale = par_ref[1:2, at]
         expo = par_ref[2:3, at]
         half = 0.5 * expo
         tails = jnp.zeros((8, BLK), jnp.float32)
         vars_ = jnp.zeros((8, BLK), jnp.float32)
-        for c in range(0, scen, STRIP):
+        for c in range(0, here, STRIP):
             strip = slice(c, c + STRIP)
             z = shift + scale * score_ref[b % slots, strip, :]
             t = pl.reciprocal(z + SHIFT, approx=True)
@@ -159,63 +178,78 @@
             far = (h * t) * (jnp.exp2((z * z) * -LOG2E) * expo)
             lost = jnp.where(z > FAR, far, half - half * lax.erf(z))
             high = lost.astype(jnp.bfloat16)
-            lost_ref[b % slots, strip, 0:BLK] = high
-            lost_ref[b % slots, strip, BLK:] = (lost - high.astype(jnp.float32)).astype(jnp.bfloat16)
-            tails += jnp.sum((lost * mark_ref[0, strip, :]).reshape(STRIP // 8, 8, BLK), axis=0)
-            vars_ += jnp.sum((lost * mark_ref[1, strip, :]).reshape(STRIP // 8, 8, BLK), axis=0)
-        con_ref[b : b + 1, :] = jnp.sum(tails, axis=0, keepdims=True) * (16.0 / scen)
-        varc_ref[b : b + 1, :] = jnp.sum(vars_, axis=0, keepdims=True)
-
-    def place(b):
-        region = where_ref[:, b * BLK : (b + 1) * BLK]
+            lost_ref[b // TOGETHER % batches, strip, to : to + BLK] = high
+            lost_ref[b // TOGETHER % batches, strip, to_low : to_low + BLK] = (
+                lost - high.astype(jnp.float32)
+            ).astype(jnp.bfloat16)
+            tails += jnp.sum((lost * part_ref[0, strip, :]).reshape(STRIP // 8, 8, BLK), axis=0)
+            vars_ += jnp.sum((lost * part_ref[1, strip, :]).reshape(STRIP // 8, 8, BLK), axis=0)
+        con_ref[b : b + 1, :] = con_in[b : b + 1, :] + jnp.sum(tails, axis=0, keepdims=True) * (16.0 / scen)
+        varc_ref[b : b + 1, :] = var_in[b : b + 1, :] + jnp.sum(vars_, axis=0, keepdims=True)
+
+    def place(batch):
+        region = where_ref[:, batch * TOGETHER * BLK : (batch + 1) * TOGETHER * BLK]
         return lax.dot_general(
-            lost_ref[b % slots], jnp.concatenate([region, region], axis=1), NT, preferred_element_type=jnp.float32
+            lost_ref[batch % batches], jnp.concatenate([region, region], axis=1), NT, preferred_element_type=jnp.float32
         )
 
-    total = jnp.zeros((scen, BLK), jnp.float32)
+    total = jnp.zeros((here, R), jnp.float32)
     for b in range(blocks + 2):
         if b < blocks:
             score(b)
         if 1 <= b <= blocks:
             weigh(b - 1)
-        if 2 <= b:
-            total += place(b - 2)
-    lane = lax.broadcasted_iota(jnp.int32, (scen, BLK), 1) // R
-    kept = jnp.where(lane == lax.broadcasted_iota(jnp.int32, (scen, BLK), 0) % GROUPS, total, 0.0)
-    loss_ref[...] = jnp.sum(kept.reshape(scen // GROUPS, GROUPS, BLK), axis=1).reshape(loss_ref.shape)
-
-
-def losses(n, pattern, own, other, loadings, params, where, marks):
-    rows = loadings.shape[0]
-    scen = 2 * own.shape[0]
+        if 2 <= b and (b - 1) % TOGETHER == 0:
+            total += place((b - 2) // TOGETHER)
+    total = jnp.concatenate([total] * GROUPS, axis=1)
+    lane = lax.broadcasted_iota(jnp.int32, (here, BLK), 1) // R
+    kept = jnp.where(lane == lax.broadcasted_iota(jnp.int32, (here, BLK), 0) % GROUPS, total, 0.0)
+    kept = jnp.sum(kept.reshape(here // GROUPS, GROUPS, BLK), axis=1)
+    if not last:
+        loss_ref[...] = kept
+        return
+    high = mine // GROUPS
+    for value, first in ((kept, bits), *zip(earlier, last)):
+        for p in range(value.shape[0] // high):
+            loss_ref[me ^ (gathered_from(p, n) | first)] = value[p * high : (p + 1) * high, :]
+
+
+def weigh(n, bits, operands, sums, factors, earlier=(), last=()):
+    pattern, turned, params, where, marks = operands
+    scen = marks.shape[1]
+    here = factors.shape[0]
+    blocks = turned.shape[0]
+    rows = blocks * BLK
     vmem = pl.BlockSpec(memory_space=pltpu.VMEM)
-    hbm = pl.BlockSpec(memory_space=pltpu.HBM)
-    return pl.pallas_call(
-        functools.partial(losses_kernel, n),
-        out_shape=(
-            jax.ShapeDtypeStruct((n, scen // n // GROUPS, BLK), jnp.float32),
-            jax.ShapeDtypeStruct((rows // BLK, BLK), jnp.float32),
-            jax.ShapeDtypeStruct((rows // BLK, BLK), jnp.float32),
-        ),
-        in_specs=[hbm] + [vmem] * 6,
+    if last:
+        loss = jax.ShapeDtypeStruct((n, scen // n // GROUPS, BLK), jnp.float32)
+    else:
+        loss = jax.ShapeDtypeStruct((here // GROUPS, BLK), jnp.float32)
+    summed = jax.ShapeDtypeStruct((blocks, BLK), jnp.float32)
+    operands = (*operands, *sums, factors, *earlier)
+    loss, *sums = pl.pallas_call(
+        functools.partial(weigh_kernel, n, last, bits),
+        out_shape=(loss, summed, summed),
+        in_specs=[vmem] * len(operands),
         out_specs=(vmem, vmem, vmem),
         scratch_shapes=[
-            pltpu.SMEM((pattern.shape[1], pattern.shape[0]), jnp.int32),
-            pltpu.VMEM((scen, own.shape[1]), jnp.bfloat16),
-            pltpu.VMEM((3, scen, BLK), jnp.float32),
-            pltpu.VMEM((3, scen, 2 * BLK), jnp.bfloat16),
-            pltpu.SemaphoreType.DMA,
+            pltpu.VMEM((3, here, BLK), jnp.float32),
+            pltpu.VMEM((2, here, 2 * TOGETHER * BLK), jnp.bfloat16),
+            pltpu.VMEM((2, here, BLK), jnp.float32),
         ],
-        compiler_params=pltpu.CompilerParams(vmem_limit_bytes=24 << 20),
+        compiler_params=pltpu.CompilerParams(vmem_limit_bytes=16 << 20),
         cost_estimate=pl.CostEstimate(
-            flops=2 * rows * scen * 512, bytes_accessed=rows * 1024, transcendentals=3 * rows * scen
-        ),
-        name="losses",
-    )(pltpu.with_memory_space_constraint(pattern.T, pltpu.HBM), own, other, loadings, params, where, marks)
-
-
-def finish_kernel(factor, parts_ref, out_ref):
+            flops=2 * rows * here * 512, bytes_accessed=rows * 1024, transcendentals=3 * rows * here
+        ),
+        name=f"weigh{bits}",
+    )(*operands)
+    return loss, sums
+
+
+def finish_kernel(factor, parts_ref, con_in, var_in, out_ref, con_ref, varc_ref):
     mine = out_ref.shape[1]
+    con_ref[...] = con_in[...]
+    varc_ref[...] = var_in[...]
     total = jnp.sum(parts_ref[...], axis=0) * factor
     rows = jnp.concatenate(
         [jnp.broadcast_to(total[k : k + 1, :], (GROUPS, BLK)) for k in range(total.shape[0])], axis=0
@@ -229,12 +263,17 @@
     )
 
 
-def finish(parts, mine, factor):
+def finish(parts, sums, mine, factor):
+    vmem = pl.BlockSpec(memory_space=pltpu.VMEM)
+    summed = jax.ShapeDtypeStruct(sums[0].shape, jnp.float32)
     return pl.pallas_call(
         functools.partial(finish_kernel, factor),
-        out_shape=jax.ShapeDtypeStruct((R, mine), jnp.float32),
+        out_shape=(jax.ShapeDtypeStruct((R, mine), jnp.float32), summed, summed),
+        in_specs=[vmem] * 3,
+        out_specs=(vmem, vmem, vmem),
+        compiler_params=pltpu.CompilerParams(vmem_limit_bytes=4 << 20),
         name="finish",
-    )(parts)
+    )(parts, *sums)
 
 
 def local(factors, loadings, pattern, threshold, rho, exposure, region, tail_mask, var_index):
@@ -250,13 +289,35 @@
     far, prepared = lax.optimization_barrier((swapped(factors, step), prepared))
     held = jnp.concatenate([factors, far], axis=0)
     step //= 2
-    while step > 1:
+    while step > 4:
         held = jnp.concatenate([held, swapped(held, step)], axis=0)
         step //= 2
-    other = swapped(held, 1)
-    loss, con, varc = losses(n, pattern, held, other, loadings, *prepared)
+    turned = turn(loadings)
+    operands = (pattern.T, turned, *prepared)
+    zero = jnp.zeros((rows // BLK, BLK), jnp.float32)
+
+    def after(x, y):
+        return lax.optimization_barrier((x, y))
+
+    near = swapped(held, 4)
+    first, turned = after(held, turned)
+    beside = swapped(first, 1)
+    loss0, sums = weigh(n, 0, operands, (zero, zero), held)
+    near, sums = after(near, sums)
+    held = jnp.concatenate([held, near], axis=0)
+    across = swapped(held, 2)
+    loss1, sums = weigh(n, 1, operands, sums, beside)
+    near, sums = after(near, sums)
+    beside = swapped(near, 1)
+    loss4, sums = weigh(n, 4, operands, sums, near)
+    loss5, sums = weigh(n, 5, operands, sums, beside)
+    across, sums = after(across, sums)
+    corner = swapped(across, 1)
+    loss2, sums = weigh(n, 2, operands, sums, across)
+    corner, sums = after(corner, sums)
+    loss, sums = weigh(n, 3, operands, sums, corner, (loss0, loss1, loss2, loss4, loss5), (0, 1, 2, 4, 5))
     parts = lax.all_to_all(loss, "scen", 0, 0)
-    own_loss = finish(parts, mine, R / (rows * n))
+    own_loss, con, varc = finish(parts, sums, mine, R / (rows * n))
     return own_loss, con.reshape(rows), varc.reshape(rows)
 
 

time: 37.1 us -> 32.7 us (0.88)
  waiting for transfers between devices: 7.65 us -> 1.4 us
  Pallas kernels: 8.45 us -> 10.4 us
  blocking collectives: 11.8 us -> 10.7 us
  local copies, waits for them, and re-layouts: 0.03 us -> 0.82 us
    ppermute x4 -> x6, waiting for transfers between devices: 7.65 us -> 1.4 us  [swapped(): return lax.ppermute(x, 'scen', [(i, i ^ step) for i in range(n)])]
    pallas_call x2 -> x8, Pallas kernels: 5.93 us -> 7.85 us  [the longest x6 6.51 us: weigh(): pl.pallas_call(functools.partial(weigh_kernel, n, last, bits), out_shape=...]
    all_to_all x1, blocking collectives: 11.8 us -> 10.7 us  [local(): parts = lax.all_to_all(loss, 'scen', 0, 0)]
    unnamed x7, local copies, waits for them, and re-layouts: 0.02 us -> 0.81 us
    ppermute x4 -> x6, starting transfers between devices: 7.4 us -> 7.66 us  [swapped(): return lax.ppermute(x, 'scen', [(i, i ^ step) for i in range(n)])]
  transfers between devices with their start and end apart: 4 -> 6, of which waited for: 3 -> 3; matrix products, arithmetic and copies ran while one was open for 0% -> 2% of each run, Pallas kernels for 7% -> 26%
where the time goes in v3:
time: 32.7 us; the launch traced here: 32.4 us
  blocking collectives  10.7 us (33%)
  Pallas kernels  10.4 us (32%)
  starting transfers between devices  7.66 us (23%)
  between operations  1.41 us (4%)
  waiting for transfers between devices  1.4 us (4%)
  local copies, waits for them, and re-layouts  0.82 us (3%)
    all_to_all x1, blocking collectives, local(): parts = lax.all_to_all(loss, 'scen', 0, 0)  10.7 us
    ppermute x6, starting transfers between devices, swapped(): return lax.ppermute(x, 'scen', [(i, i ^ step) for i in range(n)])  7.66 us
    pallas_call x6, Pallas kernels, weigh(): pl.pallas_call(functools.partial(weigh_kernel, n, last, bits), out_shape=...  6.51 us
    pallas_call x1, Pallas kernels, prepare(): pl.pallas_call(prepare_kernel, out_shape=(jax.ShapeDtypeStruct((8, rows),...  2.52 us
    ppermute x6, waiting for transfers between devices, swapped(): return lax.ppermute(x, 'scen', [(i, i ^ step) for i in range(n)])  1.4 us
    unnamed x7, local copies, waits for them, and re-layouts  0.81 us
    pallas_call x1, Pallas kernels, finish(): pl.pallas_call(functools.partial(finish_kernel, factor), out_shape=(jax.S...  0.75 us
  transfers between devices with their start and end apart: 6, of which 3 were waited for; matrix products, arithmetic and copies ran while one was open for 2% of the time, Pallas kernels for 26%

profile of v3, /device:TPU:0, one launch (start us, length us, event | category | flops | bytes accessed | tf_op | source)
XLA Modules:
  0.0 32.4 jit_solution(4375984630994022567)
XLA Ops:
  0.6 0.0 copy-start
  0.6 4.1 %collective-permute-start = (bf16[16,1024]{1,0:T(8,128)(2,1)}, bf16[16,1024]{1,0:T(8,128)(2,1)S(1)}, u32[]{:S(2)}, u32[]{:S(2)}) collective-permute-start(bf16[16,1024]{1,0:T(8,128)(2,1)} %param.9), channel_id=1, source_target_pairs={{0,8},{1,9},{2,10},{3,11},{4,12},{5,13},{6,14},{7,15},{8,0},{9,1},... | collective-permute-start | bytes 98312 | tf_op jit(solution)/shard_map/ppermute | solution.py:285
  4.7 0.8 %constant_dynamic-update-slice_fusion.1 = bf16[32,1024]{1,0:T(8,128)(2,1)S(1)} fusion(bf16[16,1024]{1,0:T(8,128)(2,1)} %param.9), kind=kLoop, calls=%fused_computation.2 | loop fusion | bytes 65536
  6.2 2.5 %prepare.1 = (f32[8,2048]{1,0:T(8,128)S(1)}, bf16[16,2048]{1,0:T(8,128)(2,1)S(1)}, f32[2,256,128]{2,1,0:T(8,128)S(1)}) custom-call(s32[8,128]{1,0:T(8,128)S(1)} %broadcast_in_dim.27.var_ref, bf16[2048,512]{1,0:T(8,128)(2,1)} %load_hbm.1, f32[1,2048]{1,0:T(1,128)} %bitcast.16, f32[1,2048]{1,0:T(1,128)} %bitcast.17, f32[1,2048]{1,0:T(1,128)} %bitcast.18, ...), custom_call_target="tpu_custom_call" | custom-call | flops 268435456 | bytes 3145728 | tf_op jit(solution)/shard_map/prepare/pallas_call | solution.py:86
  8.7 0.0 collective-permute-done
  8.7 0.0 copy-start.1
  8.8 1.6 %collective-permute-start.1 = (bf16[32,1024]{1,0:T(8,128)(2,1)S(1)}, bf16[32,1024]{1,0:T(8,128)(2,1)S(1)}, u32[]{:S(2)}, u32[]{:S(2)}) collective-permute-start(bf16[32,1024]{1,0:T(8,128)(2,1)S(1)} %constant_dynamic-update-slice_fusion.refs_7_), channel_id=1, source_target_pairs={{0,4},{1,5},{2,6},{3,7},{4,0},{5,1},{6,2},{7,3},{8,12},{9,13},{10,... | collective-permute-start | bytes 196616 | tf_op jit(solution)/shard_map/ppermute | solution.py:285
  10.4 0.0 copy-done
  10.4 0.6 %turn.1.refs_1_ = bf16[16,512,128]{2,1,0:T(8,128)(2,1)S(1)} custom-call(bf16[2048,512]{1,0:T(8,128)(2,1)S(1)} %copy-done), custom_call_target="tpu_custom_call" | custom-call | bytes 4194304 | tf_op jit(solution)/shard_map/turn/pallas_call | solution.py:125
  11.0 0.0 copy-start.2
  11.0 0.1 collective-permute-start.3
  11.1 0.0 copy-done.1
  11.1 1.0 %weigh0.1 = (f32[4,128]{1,0:T(4,128)S(1)}, f32[16,128]{1,0:T(8,128)S(1)}, f32[16,128]{1,0:T(8,128)S(1)}) custom-call(s32[4,16]{1,0:T(4,128)S(1)} %bitcast.10, bf16[16,512,128]{2,1,0:T(8,128)(2,1)S(1)} %turn.1.refs_1_, f32[8,2048]{1,0:T(8,128)S(1)} %get-tuple-element.47.refs_2_, bf16[16,2048]{1,0:T(8,128)(2,1)S(1)} %get-tuple-element.48.refs_3_, ...), custom_call_target="tpu_custom_call" | custom-call | flops 67108864 | bytes 2097152 | tf_op jit(solution)/shard_map/weigh0/pallas_call | solution.py:230
  12.1 1.0 %collective-permute-done.1.refs_7_ = bf16[32,1024]{1,0:T(8,128)(2,1)S(1)} collective-permute-done((bf16[32,1024]{1,0:T(8,128)(2,1)S(1)}, bf16[32,1024]{1,0:T(8,128)(2,1)S(1)}, u32[]{:S(2)}, u32[]{:S(2)}) %collective-permute-start.1) | collective-permute-done | bytes 65568 | tf_op jit(solution)/shard_map/ppermute | solution.py:285
  13.1 0.0 copy-done.2
  13.1 1.6 %collective-permute-start.2 = (bf16[64,1024]{1,0:T(8,128)(2,1)S(1)}, bf16[64,1024]{1,0:T(8,128)(2,1)S(1)}, u32[]{:S(2)}, u32[]{:S(2)}) collective-permute-start(bf16[64,1024]{1,0:T(8,128)(2,1)S(1)} %pad_maximum_fusion), channel_id=1, source_target_pairs={{0,2},{1,3},{2,0},{3,1},{4,6},{5,7},{6,4},{7,5},{8,10},{9,11},{10,... | collective-permute-start | bytes 393224 | tf_op jit(solution)/shard_map/ppermute | solution.py:285
  14.7 0.0 collective-permute-done.3.refs_7_
  14.7 1.0 %weigh1.1 = (f32[4,128]{1,0:T(4,128)S(1)}, f32[16,128]{1,0:T(8,128)S(1)}, f32[16,128]{1,0:T(8,128)S(1)}) custom-call(s32[4,16]{1,0:T(4,128)S(1)} %bitcast.11, bf16[16,512,128]{2,1,0:T(8,128)(2,1)S(1)} %turn.1.refs_1_, f32[8,2048]{1,0:T(8,128)S(1)} %get-tuple-element.47.refs_2_, bf16[16,2048]{1,0:T(8,128)(2,1)S(1)} %get-tuple-element.48.refs_3_, ...), custom_call_target="tpu_custom_call" | custom-call | flops 67108864 | bytes 2097152 | tf_op jit(solution)/shard_map/weigh1/pallas_call | solution.py:230
  15.7 0.1 collective-permute-start.4
  15.8 1.0 %weigh4.1 = (f32[4,128]{1,0:T(4,128)S(1)}, f32[16,128]{1,0:T(8,128)S(1)}, f32[16,128]{1,0:T(8,128)S(1)}) custom-call(s32[4,16]{1,0:T(4,128)S(1)} %bitcast.12, bf16[16,512,128]{2,1,0:T(8,128)(2,1)S(1)} %turn.1.refs_1_, f32[8,2048]{1,0:T(8,128)S(1)} %get-tuple-element.47.refs_2_, bf16[16,2048]{1,0:T(8,128)(2,1)S(1)} %get-tuple-element.48.refs_3_, ...), custom_call_target="tpu_custom_call" | custom-call | flops 67108864 | bytes 2097152 | tf_op jit(solution)/shard_map/weigh4/pallas_call | solution.py:230
  16.8 0.2 collective-permute-done.4.refs_7_
  17.0 1.0 %weigh5.1 = (f32[4,128]{1,0:T(4,128)S(1)}, f32[16,128]{1,0:T(8,128)S(1)}, f32[16,128]{1,0:T(8,128)S(1)}) custom-call(s32[4,16]{1,0:T(4,128)S(1)} %bitcast.13, bf16[16,512,128]{2,1,0:T(8,128)(2,1)S(1)} %turn.1.refs_1_, f32[8,2048]{1,0:T(8,128)S(1)} %get-tuple-element.47.refs_2_, bf16[16,2048]{1,0:T(8,128)(2,1)S(1)} %get-tuple-element.48.refs_3_, ...), custom_call_target="tpu_custom_call" | custom-call | flops 67108864 | bytes 2097152 | tf_op jit(solution)/shard_map/weigh5/pallas_call | solution.py:230
  18.0 0.1 collective-permute-done.2.refs_7_
  18.1 0.2 collective-permute-start.5
  18.3 1.3 %weigh2.1 = (f32[8,128]{1,0:T(8,128)S(1)}, f32[16,128]{1,0:T(8,128)S(1)}, f32[16,128]{1,0:T(8,128)S(1)}) custom-call(s32[4,16]{1,0:T(4,128)S(1)} %bitcast.14, bf16[16,512,128]{2,1,0:T(8,128)(2,1)S(1)} %turn.1.refs_1_, f32[8,2048]{1,0:T(8,128)S(1)} %get-tuple-element.47.refs_2_, bf16[16,2048]{1,0:T(8,128)(2,1)S(1)} %get-tuple-element.48.refs_3_, ...), custom_call_target="tpu_custom_call" | custom-call | flops 134217728 | bytes 2097152 | tf_op jit(solution)/shard_map/weigh2/pallas_call | solution.py:230
  19.7 0.0 collective-permute-done.5.refs_7_
  19.7 1.2 %weigh3.1 = (f32[16,2,128]{2,1,0:T(2,128)S(1)}, f32[16,128]{1,0:T(8,128)S(1)}, f32[16,128]{1,0:T(8,128)S(1)}) custom-call(s32[4,16]{1,0:T(4,128)S(1)} %bitcast.15, bf16[16,512,128]{2,1,0:T(8,128)(2,1)S(1)} %turn.1.refs_1_, f32[8,2048]{1,0:T(8,128)S(1)} %get-tuple-element.47.refs_2_, bf16[16,2048]{1,0:T(8,128)(2,1)S(1)} %get-tuple-element.48.refs_3_, ...), custom_call_target="tpu_custom_call" | custom-call | flops 134217728 | bytes 2097152 | tf_op jit(solution)/shard_map/weigh3/pallas_call | solution.py:230
  20.9 10.7 %all_to_all.5.parts_ref = f32[16,2,128]{2,1,0:T(2,128)S(1)} all-to-all(f32[16,2,128]{2,1,0:T(2,128)S(1)} %get-tuple-element.79), channel_id=1, replica_groups=mesh['groups'=2,'scen'=16] {'scen'}, dimensions={0} | all-to-all | bytes 32768 | tf_op jit(solution)/shard_map/all_to_all | solution.py:319
  31.7 0.7 %finish.1 = (f32[16,16]{1,0:T(8,128)}, f32[16,128]{1,0:T(8,128)}, f32[16,128]{1,0:T(8,128)}) custom-call(f32[16,2,128]{2,1,0:T(2,128)S(1)} %all_to_all.5.parts_ref, f32[16,128]{1,0:T(8,128)S(1)} %get-tuple-element.80.con_in, f32[16,128]{1,0:T(8,128)S(1)} %get-tuple-element.81.var_in), custom_call_target="tpu_custom_call" | custom-call | tf_op jit(solution)/shard_map/finish/pallas_call | solution.py:269
  (4 shorter events, 0.0 us)
Async XLA Ops:
  0.6 9.8 %copy-start = (bf16[2048,512]{1,0:T(8,128)(2,1)S(1)}, bf16[2048,512]{1,0:T(8,128)(2,1)}, u32[]{:S(2)}) copy-start(bf16[2048,512]{1,0:T(8,128)(2,1)} %load_hbm.1) | copy-start | bytes 6291460
  0.6 8.1 %collective-permute-start = (bf16[16,1024]{1,0:T(8,128)(2,1)}, bf16[16,1024]{1,0:T(8,128)(2,1)S(1)}, u32[]{:S(2)}, u32[]{:S(2)}) collective-permute-start(bf16[16,1024]{1,0:T(8,128)(2,1)} %param.9), channel_id=1, source_target_pairs={{0,8},{1,9},{2,10},{3,11},{4,12},{5,13},{6,14},{7,15},{8,0},{9,1},... | collective-permute-start | bytes 98312 | tf_op jit(solution)/shard_map/ppermute | solution.py:285
  8.7 2.4 %copy-start.1 = (s32[16,4]{0,1:T(4,128)S(1)}, s32[16,4]{0,1:T(4,128)}, u32[]{:S(2)}) copy-start(s32[16,4]{0,1:T(4,128)} %param.11) | copy-start | bytes 772
  8.8 4.3 %collective-permute-start.1 = (bf16[32,1024]{1,0:T(8,128)(2,1)S(1)}, bf16[32,1024]{1,0:T(8,128)(2,1)S(1)}, u32[]{:S(2)}, u32[]{:S(2)}) collective-permute-start(bf16[32,1024]{1,0:T(8,128)(2,1)S(1)} %constant_dynamic-update-slice_fusion.refs_7_), channel_id=1, source_target_pairs={{0,4},{1,5},{2,6},{3,7},{4,0},{5,1},{6,2},{7,3},{8,12},{9,13},{10,... | collective-permute-start | bytes 196616 | tf_op jit(solution)/shard_map/ppermute | solution.py:285
  11.0 2.1 %copy-start.2 = (bf16[16,1024]{1,0:T(8,128)(2,1)S(1)}, bf16[16,1024]{1,0:T(8,128)(2,1)}, u32[]{:S(2)}) copy-start(bf16[16,1024]{1,0:T(8,128)(2,1)} %param.9) | copy-start | bytes 98308
  11.0 3.7 %collective-permute-start.3 = (bf16[32,1024]{1,0:T(8,128)(2,1)S(1)}, bf16[32,1024]{1,0:T(8,128)(2,1)S(1)}, u32[]{:S(2)}, u32[]{:S(2)}) collective-permute-start(bf16[32,1024]{1,0:T(8,128)(2,1)S(1)} %constant_dynamic-update-slice_fusion.refs_7_), channel_id=1, source_target_pairs={{0,1},{1,0},{2,3},{3,2},{4,5},{5,4},{6,7},{7,6},{8,9},{9,8},{10,11... | collective-permute-start | bytes 196616 | tf_op jit(solution)/shard_map/ppermute | solution.py:285
  13.1 5.0 %collective-permute-start.2 = (bf16[64,1024]{1,0:T(8,128)(2,1)S(1)}, bf16[64,1024]{1,0:T(8,128)(2,1)S(1)}, u32[]{:S(2)}, u32[]{:S(2)}) collective-permute-start(bf16[64,1024]{1,0:T(8,128)(2,1)S(1)} %pad_maximum_fusion), channel_id=1, source_target_pairs={{0,2},{1,3},{2,0},{3,1},{4,6},{5,7},{6,4},{7,5},{8,10},{9,11},{10,... | collective-permute-start | bytes 393224 | tf_op jit(solution)/shard_map/ppermute | solution.py:285
  15.7 1.3 %collective-permute-start.4 = (bf16[32,1024]{1,0:T(8,128)(2,1)S(1)}, bf16[32,1024]{1,0:T(8,128)(2,1)S(1)}, u32[]{:S(2)}, u32[]{:S(2)}) collective-permute-start(bf16[32,1024]{1,0:T(8,128)(2,1)S(1)} %collective-permute-done.1.refs_7_), channel_id=1, source_target_pairs={{0,1},{1,0},{2,3},{3,2},{4,5},{5,4},{6,7},{7,6},{8,9},{9,8},{10,11... | collective-permute-start | bytes 196616 | tf_op jit(solution)/shard_map/ppermute | solution.py:285
  18.1 1.5 %collective-permute-start.5 = (bf16[64,1024]{1,0:T(8,128)(2,1)S(1)}, bf16[64,1024]{1,0:T(8,128)(2,1)S(1)}, u32[]{:S(2)}, u32[]{:S(2)}) collective-permute-start(bf16[64,1024]{1,0:T(8,128)(2,1)S(1)} %collective-permute-done.2.refs_7_), channel_id=1, source_target_pairs={{0,1},{1,0},{2,3},{3,2},{4,5},{5,4},{6,7},{7,6},{8,9},{9,8},{10,11... | collective-permute-start | bytes 393224 | tf_op jit(solution)/shard_map/ppermute | solution.py:285

commit v4 on v3

--- a/solution.py
+++ b/solution.py
@@ -12,6 +12,7 @@
 BLK = 128
 GROUPS = BLK // R
 STRIP = 32
+COST = pl.CostEstimate(flops=2 * 10**9, bytes_accessed=0, transcendentals=0)
 TOGETHER = 4
 NT = (((1,), (1,)), ((), ()))
 LOG2E = math.log2(math.e)
@@ -36,25 +37,23 @@
 
 
 def prepare_kernel(
-    var_ref, load_hbm, thr_hbm, rho_hbm, expo_hbm, region_hbm, tail_hbm, par_ref, where_ref, mark_ref,
-    load_ref, thr_ref, rho_ref, expo_ref, region_ref, tail_ref, sems,
+    var_ref, load_hbm, thr_hbm, rho_hbm, expo_hbm, region_hbm, tail_hbm, load_ref, par_ref, where_ref, mark_ref,
+    thr_ref, rho_ref, expo_ref, region_ref, tail_ref, sems,
 ):
-    rows, width = load_ref.shape
+    rows = load_ref.shape[0]
     pairs = (
         (thr_hbm, thr_ref), (rho_hbm, rho_ref), (expo_hbm, expo_ref), (region_hbm, region_ref), (tail_hbm, tail_ref),
     )
     copies = [pltpu.make_async_copy(a, b, sems.at[i]) for i, (a, b) in enumerate(pairs)]
     parts = 4
-    piece = rows // parts
     for i in range(parts):
-        at = pl.ds(i * piece, piece)
+        at = pl.ds(i * rows // parts, rows // parts)
         copies.append(pltpu.make_async_copy(load_hbm.at[at, :], load_ref.at[at, :], sems.at[len(pairs) + i]))
     for copy in copies:
         copy.start()
     for copy in copies[: len(pairs)]:
         copy.wait()
     scen = tail_ref.shape[1]
-    diagonal = lax.broadcasted_iota(jnp.int32, (BLK, BLK), 0) == lax.broadcasted_iota(jnp.int32, (BLK, BLK), 1)
     for c in range(scen // BLK):
         at = slice(c * BLK, (c + 1) * BLK)
         tail = jnp.where(tail_ref[:, at] == 1, 1.0, 0.0)
@@ -64,19 +63,14 @@
     row_region = lax.broadcasted_iota(jnp.int32, (R, rows), 0)
     where_ref[...] = jnp.where(row_region == region_ref[...], 1.0, 0.0).astype(jnp.bfloat16)
     par_ref[...] = jnp.zeros_like(par_ref)
-    for i in range(parts):
-        copies[len(pairs) + i].wait()
-        for b in range(i * piece // BLK, (i + 1) * piece // BLK):
-            at = slice(b * BLK, (b + 1) * BLK)
-            block = load_ref[at, :]
-            gram = lax.dot_general(block, block, NT, preferred_element_type=jnp.float32)
-            mean_sq = jnp.sum(jnp.where(diagonal, gram, 0.0), axis=0, keepdims=True) * (1.0 / width)
-            rho = rho_ref[:, at]
-            scale = jnp.sqrt(rho / (width * (mean_sq + 1e-06)))
-            to_z = math.sqrt(0.5) / jnp.sqrt(1.0 - rho)
-            par_ref[0:1, at] = -thr_ref[:, at] * to_z
-            par_ref[1:2, at] = scale * to_z
-            par_ref[2:3, at] = expo_ref[:, at]
+    rho = rho_ref[...]
+    to_z = math.sqrt(0.5) / jnp.sqrt(1.0 - rho)
+    par_ref[0:1, :] = -thr_ref[...] * to_z
+    par_ref[1:2, :] = to_z
+    par_ref[2:3, :] = expo_ref[...]
+    par_ref[3:4, :] = rho
+    for copy in copies[len(pairs) :]:
+        copy.wait()
 
 
 def prepare(loadings, threshold, rho, exposure, region, tail_mask, var_index):
@@ -86,13 +80,13 @@
     return pl.pallas_call(
         prepare_kernel,
         out_shape=(
+            jax.ShapeDtypeStruct(loadings.shape, loadings.dtype),
             jax.ShapeDtypeStruct((8, rows), jnp.float32),
             jax.ShapeDtypeStruct((R, rows), jnp.bfloat16),
             jax.ShapeDtypeStruct((2, scen, BLK), jnp.float32),
         ),
         in_specs=[pl.BlockSpec(memory_space=pltpu.VMEM)] + [hbm] * 6,
         scratch_shapes=[
-            pltpu.VMEM(loadings.shape, loadings.dtype),
             pltpu.VMEM((1, rows), jnp.float32),
             pltpu.VMEM((1, rows), jnp.float32),
             pltpu.VMEM((1, rows), jnp.float32),
@@ -101,9 +95,7 @@
             pltpu.SemaphoreType.DMA((9,)),
         ],
         compiler_params=pltpu.CompilerParams(vmem_limit_bytes=16 << 20),
-        cost_estimate=pl.CostEstimate(
-            flops=2 * rows * BLK * loadings.shape[1], bytes_accessed=3 * rows * 512, transcendentals=2 * rows
-        ),
+        cost_estimate=COST,
         name="prepare",
     )(
         jnp.broadcast_to(var_index[None], (8, BLK)),
@@ -114,27 +106,40 @@
     )
 
 
-def turn_kernel(load_ref, turned_ref):
+def turn_kernel(load_ref, par_in, turned_ref, par_ref):
+    width = load_ref.shape[1]
+    diagonal = lax.broadcasted_iota(jnp.int32, (BLK, BLK), 0) == lax.broadcasted_iota(jnp.int32, (BLK, BLK), 1)
+    par_ref[...] = par_in[...]
     for b in range(turned_ref.shape[0]):
-        turned_ref[b] = load_ref[b * BLK : (b + 1) * BLK, :].T
-
-
-def turn(loadings):
+        at = slice(b * BLK, (b + 1) * BLK)
+        block = load_ref[at, :]
+        turned = block.T
+        turned_ref[b] = turned
+        gram = jnp.dot(block, turned, preferred_element_type=jnp.float32)
+        mean_sq = jnp.sum(jnp.where(diagonal, gram, 0.0), axis=0, keepdims=True) * (1.0 / width)
+        par_ref[1:2, at] = par_in[1:2, at] * jnp.sqrt(par_in[3:4, at] / (width * (mean_sq + 1e-06)))
+
+
+def turn(loadings, params):
     rows, width = loadings.shape
     vmem = pl.BlockSpec(memory_space=pltpu.VMEM)
     return pl.pallas_call(
         turn_kernel,
-        out_shape=jax.ShapeDtypeStruct((rows // BLK, width, BLK), loadings.dtype),
-        in_specs=[vmem],
-        out_specs=vmem,
+        out_shape=(
+            jax.ShapeDtypeStruct((rows // BLK, width, BLK), loadings.dtype),
+            jax.ShapeDtypeStruct(params.shape, params.dtype),
+        ),
+        in_specs=[vmem, vmem],
+        out_specs=(vmem, vmem),
         compiler_params=pltpu.CompilerParams(vmem_limit_bytes=16 << 20),
-        cost_estimate=pl.CostEstimate(flops=0, bytes_accessed=4 * rows * width, transcendentals=0),
+        cost_estimate=COST,
         name="turn",
-    )(loadings)
+    )(loadings, params)
 
 
 def gathered_from(p, n):
-    return 4 * flipped(p, n // 4)
+    q, low = divmod(p, 4)
+    return 16 * flipped(q, n // 16) ^ 4 * low
 
 
 def weigh_kernel(n, last, bits, *refs):
@@ -238,9 +243,7 @@
             pltpu.VMEM((2, here, BLK), jnp.float32),
         ],
         compiler_params=pltpu.CompilerParams(vmem_limit_bytes=16 << 20),
-        cost_estimate=pl.CostEstimate(
-            flops=2 * rows * here * 512, bytes_accessed=rows * 1024, transcendentals=3 * rows * here
-        ),
+        cost_estimate=COST,
         name=f"weigh{bits}",
     )(*operands)
     return loss, sums
@@ -284,38 +287,37 @@
     def swapped(x, step):
         return lax.ppermute(x, "scen", [(i, i ^ step) for i in range(n)])
 
+    def after(x, y):
+        return lax.optimization_barrier((x, y))
+
+    held = factors
     step = n // 2
-    prepared = prepare(loadings, threshold, rho, exposure, region, tail_mask, var_index)
-    far, prepared = lax.optimization_barrier((swapped(factors, step), prepared))
-    held = jnp.concatenate([factors, far], axis=0)
-    step //= 2
-    while step > 4:
+    while step > 8:
         held = jnp.concatenate([held, swapped(held, step)], axis=0)
         step //= 2
-    turned = turn(loadings)
-    operands = (pattern.T, turned, *prepared)
+    prepared = prepare(loadings, threshold, rho, exposure, region, tail_mask, var_index)
+    o8 = swapped(held, 8)
+    o12 = swapped(held, 12)
+    o4 = swapped(held, 4)
+    (o8, o12, o4), prepared = after((o8, o12, o4), prepared)
+    others = [o4, o8, o12]
+    shape = (-1, 1, mine, factors.shape[1])
+    held = jnp.concatenate([x.reshape(shape) for x in (held, *others)], axis=1).reshape(-1, factors.shape[1])
+    loadings, params, where, marks = prepared
+    turned, params = turn(loadings, params)
+    operands = (pattern.T, turned, params, where, marks)
     zero = jnp.zeros((rows // BLK, BLK), jnp.float32)
 
-    def after(x, y):
-        return lax.optimization_barrier((x, y))
-
-    near = swapped(held, 4)
+    across = swapped(held, 2)
     first, turned = after(held, turned)
     beside = swapped(first, 1)
     loss0, sums = weigh(n, 0, operands, (zero, zero), held)
-    near, sums = after(near, sums)
-    held = jnp.concatenate([held, near], axis=0)
-    across = swapped(held, 2)
     loss1, sums = weigh(n, 1, operands, sums, beside)
-    near, sums = after(near, sums)
-    beside = swapped(near, 1)
-    loss4, sums = weigh(n, 4, operands, sums, near)
-    loss5, sums = weigh(n, 5, operands, sums, beside)
     across, sums = after(across, sums)
     corner = swapped(across, 1)
     loss2, sums = weigh(n, 2, operands, sums, across)
     corner, sums = after(corner, sums)
-    loss, sums = weigh(n, 3, operands, sums, corner, (loss0, loss1, loss2, loss4, loss5), (0, 1, 2, 4, 5))
+    loss, sums = weigh(n, 3, operands, sums, corner, (loss0, loss1, loss2), (0, 1, 2))
     parts = lax.all_to_all(loss, "scen", 0, 0)
     own_loss, con, varc = finish(parts, sums, mine, R / (rows * n))
     return own_loss, con.reshape(rows), varc.reshape(rows)

time: 32.7 us -> 30 us (0.917)
  Pallas kernels: 10.4 us -> 8.41 us
  local copies, waits for them, and re-layouts: 0.82 us -> 0.02 us
  blocking collectives: 10.7 us -> 10.1 us
  waiting for transfers between devices: 1.4 us -> 1.98 us
    pallas_call x6 -> x4, Pallas kernels: 6.51 us -> 5.19 us  [weigh(): pl.pallas_call(functools.partial(weigh_kernel, n, last, bits), out_shape=...]
    unnamed x7 -> x4, local copies, waits for them, and re-layouts: 0.81 us -> 0.01 us
    pallas_call x2, Pallas kernels: 3.11 us -> 2.47 us  [the longest x1 1.68 us: prepare(): pl.pallas_call(prepare_kernel, out_shape=(jax.ShapeDtypeStruct(loadings.s...]
    all_to_all x1, blocking collectives: 10.7 us -> 10.1 us  [local(): parts = lax.all_to_all(loss, 'scen', 0, 0)]
    ppermute x6, waiting for transfers between devices: 1.4 us -> 1.98 us  [swapped(): return lax.ppermute(x, 'scen', [(i, i ^ step) for i in range(n)])]
  transfers between devices with their start and end apart: 6 -> 6, of which waited for: 3 -> 1; matrix products, arithmetic and copies ran while one was open for 2% -> 0% of each run, Pallas kernels for 26% -> 22%
where the time goes in v4:
time: 30 us; the launch traced here: 29.8 us
  blocking collectives  10.1 us (34%)
  Pallas kernels  8.41 us (28%)
  starting transfers between devices  7.88 us (26%)
  waiting for transfers between devices  1.98 us (7%)
  between operations  1.4 us (5%)
    all_to_all x1, blocking collectives, local(): parts = lax.all_to_all(loss, 'scen', 0, 0)  10.1 us
    ppermute x6, starting transfers between devices, swapped(): return lax.ppermute(x, 'scen', [(i, i ^ step) for i in range(n)])  7.88 us
    pallas_call x4, Pallas kernels, weigh(): pl.pallas_call(functools.partial(weigh_kernel, n, last, bits), out_shape=...  5.19 us
    ppermute x6, waiting for transfers between devices, swapped(): return lax.ppermute(x, 'scen', [(i, i ^ step) for i in range(n)])  1.98 us
    pallas_call x1, Pallas kernels, prepare(): pl.pallas_call(prepare_kernel, out_shape=(jax.ShapeDtypeStruct(loadings.s...  1.68 us
    pallas_call x1, Pallas kernels, turn(): pl.pallas_call(turn_kernel, out_shape=(jax.ShapeDtypeStruct((rows // BLK,...  0.79 us
    pallas_call x1, Pallas kernels, finish(): pl.pallas_call(functools.partial(finish_kernel, factor), out_shape=(jax.S...  0.75 us
  transfers between devices with their start and end apart: 6, of which 1 were waited for; matrix products, arithmetic and copies ran while one was open for 0% of the time, Pallas kernels for 22%

profile of v4, /device:TPU:0, one launch (start us, length us, event | category | flops | bytes accessed | tf_op | source)
XLA Modules:
  0.0 29.8 jit_solution(15843099150663286822)
XLA Ops:
  0.6 4.1 %collective-permute-start = (bf16[16,1024]{1,0:T(8,128)(2,1)}, bf16[16,1024]{1,0:T(8,128)(2,1)S(1)}, u32[]{:S(2)}, u32[]{:S(2)}) collective-permute-start(bf16[16,1024]{1,0:T(8,128)(2,1)} %param.9), channel_id=1, source_target_pairs={{0,8},{1,9},{2,10},{3,11},{4,12},{5,13},{6,14},{7,15},{8,0},{9,1},... | collective-permute-start | bytes 98312 | tf_op jit(solution)/shard_map/ppermute | solution.py:288
  4.7 1.3 %collective-permute-start.1 = (bf16[16,1024]{1,0:T(8,128)(2,1)}, bf16[16,1024]{1,0:T(8,128)(2,1)S(1)}, u32[]{:S(2)}, u32[]{:S(2)}) collective-permute-start(bf16[16,1024]{1,0:T(8,128)(2,1)} %param.9), channel_id=1, source_target_pairs={{0,12},{1,13},{2,14},{3,15},{4,8},{5,9},{6,10},{7,11},{8,4},{9,5},... | collective-permute-start | bytes 98312 | tf_op jit(solution)/shard_map/ppermute | solution.py:288
  6.1 0.2 collective-permute-start.2
  7.0 0.0 copy-start.1
  7.0 1.7 %prepare.1 = (bf16[2048,512]{1,0:T(8,128)(2,1)S(1)}, f32[8,2048]{1,0:T(8,128)S(1)}, bf16[16,2048]{1,0:T(8,128)(2,1)S(1)}, f32[2,256,128]{2,1,0:T(8,128)S(1)}) custom-call(s32[8,128]{1,0:T(8,128)S(1)} %broadcast_in_dim.27.var_ref, bf16[2048,512]{1,0:T(8,128)(2,1)} %load_hbm.1, f32[1,2048]{1,0:T(1,128)} %bitcast.26, f32[1,2048]{1,0:T(1,128)} %bitcast.27, ...), custom_call_target="tpu_custom_call" | custom-call | flops 2000000000 | tf_op jit(solution)/shard_map/prepare/pallas_call | solution.py:80
  8.7 0.0 collective-permute-done
  8.7 2.0 %collective-permute-done.1 = bf16[16,1024]{1,0:T(8,128)(2,1)S(1)} collective-permute-done((bf16[16,1024]{1,0:T(8,128)(2,1)}, bf16[16,1024]{1,0:T(8,128)(2,1)S(1)}, u32[]{:S(2)}, u32[]{:S(2)}) %collective-permute-start.1) | collective-permute-done | bytes 32800 | tf_op jit(solution)/shard_map/ppermute | solution.py:288
  10.7 0.0 collective-permute-done.2
  10.7 0.0 copy-done.1
  10.7 0.0 copy-start
  10.7 1.6 %collective-permute-start.3 = (bf16[64,1024]{1,0:T(8,128)(2,1)S(1)}, bf16[64,1024]{1,0:T(8,128)(2,1)S(1)}, u32[]{:S(2)}, u32[]{:S(2)}) collective-permute-start(bf16[64,1024]{1,0:T(8,128)(2,1)S(1)} %bitcast.15), channel_id=1, source_target_pairs={{0,2},{1,3},{2,0},{3,1},{4,6},{5,7},{6,4},{7,5},{8,10},{9,11},{10,... | collective-permute-start | bytes 393224 | tf_op jit(solution)/shard_map/ppermute | solution.py:288
  12.3 0.8 %turn.1 = (bf16[16,512,128]{2,1,0:T(8,128)(2,1)S(1)}, f32[8,2048]{1,0:T(8,128)S(1)}) custom-call(bf16[2048,512]{1,0:T(8,128)(2,1)S(1)} %get-tuple-element.42.load_ref, f32[8,2048]{1,0:T(8,128)S(1)} %get-tuple-element.43.par_in), custom_call_target="tpu_custom_call" | custom-call | flops 2000000000 | tf_op jit(solution)/shard_map/turn/pallas_call | solution.py:126
  13.1 0.1 collective-permute-start.4
  13.2 0.0 copy-done
  13.2 1.3 %weigh0.1 = (f32[8,128]{1,0:T(8,128)S(1)}, f32[16,128]{1,0:T(8,128)S(1)}, f32[16,128]{1,0:T(8,128)S(1)}) custom-call(s32[4,16]{1,0:T(4,128)S(1)} %bitcast.18, bf16[16,512,128]{2,1,0:T(8,128)(2,1)S(1)} %get-tuple-element.44.refs_1_, f32[8,2048]{1,0:T(8,128)S(1)} %get-tuple-element.45.refs_2_, bf16[16,2048]{1,0:T(8,128)(2,1)S(1)} %get-tuple-element.46.refs_3_, ...), custom_call_target="tpu_custom_call" | custom-call | flops 2000000000 | tf_op jit(solution)/shard_map/weigh0/pallas_call | solution.py:235
  14.5 0.0 collective-permute-done.4.refs_7_
  14.5 1.3 %weigh1.1 = (f32[8,128]{1,0:T(8,128)S(1)}, f32[16,128]{1,0:T(8,128)S(1)}, f32[16,128]{1,0:T(8,128)S(1)}) custom-call(s32[4,16]{1,0:T(4,128)S(1)} %bitcast.19, bf16[16,512,128]{2,1,0:T(8,128)(2,1)S(1)} %get-tuple-element.44.refs_1_, f32[8,2048]{1,0:T(8,128)S(1)} %get-tuple-element.45.refs_2_, bf16[16,2048]{1,0:T(8,128)(2,1)S(1)} %get-tuple-element.46.refs_3_, ...), custom_call_target="tpu_custom_call" | custom-call | flops 2000000000 | tf_op jit(solution)/shard_map/weigh1/pallas_call | solution.py:235
  15.8 0.0 collective-permute-done.3.refs_7_
  15.8 0.5 %collective-permute-start.5 = (bf16[64,1024]{1,0:T(8,128)(2,1)S(1)}, bf16[64,1024]{1,0:T(8,128)(2,1)S(1)}, u32[]{:S(2)}, u32[]{:S(2)}) collective-permute-start(bf16[64,1024]{1,0:T(8,128)(2,1)S(1)} %collective-permute-done.3.refs_7_), channel_id=1, source_target_pairs={{0,1},{1,0},{2,3},{3,2},{4,5},{5,4},{6,7},{7,6},{8,9},{9,8},{10,11... | collective-permute-start | bytes 393224 | tf_op jit(solution)/shard_map/ppermute | solution.py:288
  16.4 1.3 %weigh2.1 = (f32[8,128]{1,0:T(8,128)S(1)}, f32[16,128]{1,0:T(8,128)S(1)}, f32[16,128]{1,0:T(8,128)S(1)}) custom-call(s32[4,16]{1,0:T(4,128)S(1)} %bitcast.20, bf16[16,512,128]{2,1,0:T(8,128)(2,1)S(1)} %get-tuple-element.44.refs_1_, f32[8,2048]{1,0:T(8,128)S(1)} %get-tuple-element.45.refs_2_, bf16[16,2048]{1,0:T(8,128)(2,1)S(1)} %get-tuple-element.46.refs_3_, ...), custom_call_target="tpu_custom_call" | custom-call | flops 2000000000 | tf_op jit(solution)/shard_map/weigh2/pallas_call | solution.py:235
  17.7 0.0 collective-permute-done.5.refs_7_
  17.7 1.2 %weigh3.1 = (f32[16,2,128]{2,1,0:T(2,128)S(1)}, f32[16,128]{1,0:T(8,128)S(1)}, f32[16,128]{1,0:T(8,128)S(1)}) custom-call(s32[4,16]{1,0:T(4,128)S(1)} %bitcast.21, bf16[16,512,128]{2,1,0:T(8,128)(2,1)S(1)} %get-tuple-element.44.refs_1_, f32[8,2048]{1,0:T(8,128)S(1)} %get-tuple-element.45.refs_2_, bf16[16,2048]{1,0:T(8,128)(2,1)S(1)} %get-tuple-element.46.refs_3_, ...), custom_call_target="tpu_custom_call" | custom-call | flops 2000000000 | tf_op jit(solution)/shard_map/weigh3/pallas_call | solution.py:235
  19.0 10.1 %all_to_all.5.parts_ref = f32[16,2,128]{2,1,0:T(2,128)S(1)} all-to-all(f32[16,2,128]{2,1,0:T(2,128)S(1)} %get-tuple-element.67), channel_id=1, replica_groups=mesh['groups'=2,'scen'=16] {'scen'}, dimensions={0} | all-to-all | bytes 32768 | tf_op jit(solution)/shard_map/all_to_all | solution.py:321
  29.1 0.7 %finish.1 = (f32[16,16]{1,0:T(8,128)}, f32[16,128]{1,0:T(8,128)}, f32[16,128]{1,0:T(8,128)}) custom-call(f32[16,2,128]{2,1,0:T(2,128)S(1)} %all_to_all.5.parts_ref, f32[16,128]{1,0:T(8,128)S(1)} %get-tuple-element.68.con_in, f32[16,128]{1,0:T(8,128)S(1)} %get-tuple-element.69.var_in), custom_call_target="tpu_custom_call" | custom-call | tf_op jit(solution)/shard_map/finish/pallas_call | solution.py:272
  (3 shorter events, 0.0 us)
Async XLA Ops:
  0.6 8.0 %collective-permute-start = (bf16[16,1024]{1,0:T(8,128)(2,1)}, bf16[16,1024]{1,0:T(8,128)(2,1)S(1)}, u32[]{:S(2)}, u32[]{:S(2)}) collective-permute-start(bf16[16,1024]{1,0:T(8,128)(2,1)} %param.9), channel_id=1, source_target_pairs={{0,8},{1,9},{2,10},{3,11},{4,12},{5,13},{6,14},{7,15},{8,0},{9,1},... | collective-permute-start | bytes 98312 | tf_op jit(solution)/shard_map/ppermute | solution.py:288
  4.7 5.9 %collective-permute-start.1 = (bf16[16,1024]{1,0:T(8,128)(2,1)}, bf16[16,1024]{1,0:T(8,128)(2,1)S(1)}, u32[]{:S(2)}, u32[]{:S(2)}) collective-permute-start(bf16[16,1024]{1,0:T(8,128)(2,1)} %param.9), channel_id=1, source_target_pairs={{0,12},{1,13},{2,14},{3,15},{4,8},{5,9},{6,10},{7,11},{8,4},{9,5},... | collective-permute-start | bytes 98312 | tf_op jit(solution)/shard_map/ppermute | solution.py:288
  6.1 4.6 %collective-permute-start.2 = (bf16[16,1024]{1,0:T(8,128)(2,1)}, bf16[16,1024]{1,0:T(8,128)(2,1)S(1)}, u32[]{:S(2)}, u32[]{:S(2)}) collective-permute-start(bf16[16,1024]{1,0:T(8,128)(2,1)} %param.9), channel_id=1, source_target_pairs={{0,4},{1,5},{2,6},{3,7},{4,0},{5,1},{6,2},{7,3},{8,12},{9,13},{10,... | collective-permute-start | bytes 98312 | tf_op jit(solution)/shard_map/ppermute | solution.py:288
  7.0 3.7 %copy-start.1 = (bf16[16,1024]{1,0:T(8,128)(2,1)S(1)}, bf16[16,1024]{1,0:T(8,128)(2,1)}, u32[]{:S(2)}) copy-start(bf16[16,1024]{1,0:T(8,128)(2,1)} %param.9) | copy-start | bytes 98308
  10.7 2.5 %copy-start = (s32[16,4]{0,1:T(4,128)S(1)}, s32[16,4]{0,1:T(4,128)}, u32[]{:S(2)}) copy-start(s32[16,4]{0,1:T(4,128)} %param.11) | copy-start | bytes 772
  10.7 5.1 %collective-permute-start.3 = (bf16[64,1024]{1,0:T(8,128)(2,1)S(1)}, bf16[64,1024]{1,0:T(8,128)(2,1)S(1)}, u32[]{:S(2)}, u32[]{:S(2)}) collective-permute-start(bf16[64,1024]{1,0:T(8,128)(2,1)S(1)} %bitcast.15), channel_id=1, source_target_pairs={{0,2},{1,3},{2,0},{3,1},{4,6},{5,7},{6,4},{7,5},{8,10},{9,11},{10,... | collective-permute-start | bytes 393224 | tf_op jit(solution)/shard_map/ppermute | solution.py:288
  13.1 1.4 %collective-permute-start.4 = (bf16[64,1024]{1,0:T(8,128)(2,1)S(1)}, bf16[64,1024]{1,0:T(8,128)(2,1)S(1)}, u32[]{:S(2)}, u32[]{:S(2)}) collective-permute-start(bf16[64,1024]{1,0:T(8,128)(2,1)S(1)} %bitcast.16), channel_id=1, source_target_pairs={{0,1},{1,0},{2,3},{3,2},{4,5},{5,4},{6,7},{7,6},{8,9},{9,8},{10,11... | collective-permute-start | bytes 393224 | tf_op jit(solution)/shard_map/ppermute | solution.py:288
  15.8 1.9 %collective-permute-start.5 = (bf16[64,1024]{1,0:T(8,128)(2,1)S(1)}, bf16[64,1024]{1,0:T(8,128)(2,1)S(1)}, u32[]{:S(2)}, u32[]{:S(2)}) collective-permute-start(bf16[64,1024]{1,0:T(8,128)(2,1)S(1)} %collective-permute-done.3.refs_7_), channel_id=1, source_target_pairs={{0,1},{1,0},{2,3},{3,2},{4,5},{5,4},{6,7},{7,6},{8,9},{9,8},{10,11... | collective-permute-start | bytes 393224 | tf_op jit(solution)/shard_map/ppermute | solution.py:288

commit v5 on v4

--- a/solution.py
+++ b/solution.py
@@ -37,29 +37,23 @@
 
 
 def prepare_kernel(
-    var_ref, load_hbm, thr_hbm, rho_hbm, expo_hbm, region_hbm, tail_hbm, load_ref, par_ref, where_ref, mark_ref,
+    thr_hbm, rho_hbm, expo_hbm, region_hbm, tail_hbm, par_ref, where_ref, mark_ref,
     thr_ref, rho_ref, expo_ref, region_ref, tail_ref, sems,
 ):
-    rows = load_ref.shape[0]
+    rows = par_ref.shape[1]
     pairs = (
         (thr_hbm, thr_ref), (rho_hbm, rho_ref), (expo_hbm, expo_ref), (region_hbm, region_ref), (tail_hbm, tail_ref),
     )
     copies = [pltpu.make_async_copy(a, b, sems.at[i]) for i, (a, b) in enumerate(pairs)]
-    parts = 4
-    for i in range(parts):
-        at = pl.ds(i * rows // parts, rows // parts)
-        copies.append(pltpu.make_async_copy(load_hbm.at[at, :], load_ref.at[at, :], sems.at[len(pairs) + i]))
     for copy in copies:
         copy.start()
-    for copy in copies[: len(pairs)]:
+    for copy in copies:
         copy.wait()
     scen = tail_ref.shape[1]
     for c in range(scen // BLK):
         at = slice(c * BLK, (c + 1) * BLK)
         tail = jnp.where(tail_ref[:, at] == 1, 1.0, 0.0)
-        mark_ref[0, at, :] = jnp.broadcast_to(tail, (BLK, BLK)).T
-        scenario = lax.broadcasted_iota(jnp.int32, (BLK, BLK), 0) + c * BLK
-        mark_ref[1, at, :] = jnp.where(scenario == var_ref[0:1, :], 1.0, 0.0)
+        mark_ref[at, :] = jnp.broadcast_to(tail, (BLK, BLK)).T
     row_region = lax.broadcasted_iota(jnp.int32, (R, rows), 0)
     where_ref[...] = jnp.where(row_region == region_ref[...], 1.0, 0.0).astype(jnp.bfloat16)
     par_ref[...] = jnp.zeros_like(par_ref)
@@ -69,44 +63,44 @@
     par_ref[1:2, :] = to_z
     par_ref[2:3, :] = expo_ref[...]
     par_ref[3:4, :] = rho
-    for copy in copies[len(pairs) :]:
-        copy.wait()
-
-
-def prepare(loadings, threshold, rho, exposure, region, tail_mask, var_index):
-    rows = loadings.shape[0]
+
+
+def prepare(threshold, rho, exposure, region, tail_mask):
+    rows = threshold.shape[0]
     scen = tail_mask.shape[0]
     hbm = pl.BlockSpec(memory_space=pltpu.HBM)
     return pl.pallas_call(
         prepare_kernel,
         out_shape=(
-            jax.ShapeDtypeStruct(loadings.shape, loadings.dtype),
             jax.ShapeDtypeStruct((8, rows), jnp.float32),
             jax.ShapeDtypeStruct((R, rows), jnp.bfloat16),
-            jax.ShapeDtypeStruct((2, scen, BLK), jnp.float32),
+            jax.ShapeDtypeStruct((scen, BLK), jnp.float32),
         ),
-        in_specs=[pl.BlockSpec(memory_space=pltpu.VMEM)] + [hbm] * 6,
+        in_specs=[hbm] * 5,
         scratch_shapes=[
             pltpu.VMEM((1, rows), jnp.float32),
             pltpu.VMEM((1, rows), jnp.float32),
             pltpu.VMEM((1, rows), jnp.float32),
             pltpu.VMEM((1, rows), jnp.int32),
             pltpu.VMEM((1, scen), jnp.int32),
-            pltpu.SemaphoreType.DMA((9,)),
+            pltpu.SemaphoreType.DMA((5,)),
         ],
         compiler_params=pltpu.CompilerParams(vmem_limit_bytes=16 << 20),
         cost_estimate=COST,
         name="prepare",
     )(
-        jnp.broadcast_to(var_index[None], (8, BLK)),
         *(
             pltpu.with_memory_space_constraint(x, pltpu.HBM)
-            for x in (loadings, threshold[None], rho[None], exposure[None], region[None], tail_mask[None])
+            for x in (threshold[None], rho[None], exposure[None], region[None], tail_mask[None])
         ),
     )
 
 
-def turn_kernel(load_ref, par_in, turned_ref, par_ref):
+def turn_kernel(load_ref, par_in, mark_in, var_ref, turned_ref, par_ref, mark_ref):
+    scen = mark_in.shape[0]
+    mark_ref[0] = mark_in[...]
+    scenario = lax.broadcasted_iota(jnp.int32, (scen, BLK), 0)
+    mark_ref[1] = jnp.where(scenario == var_ref[0:1, :], 1.0, 0.0)
     width = load_ref.shape[1]
     diagonal = lax.broadcasted_iota(jnp.int32, (BLK, BLK), 0) == lax.broadcasted_iota(jnp.int32, (BLK, BLK), 1)
     par_ref[...] = par_in[...]
@@ -120,7 +114,7 @@
         par_ref[1:2, at] = par_in[1:2, at] * jnp.sqrt(par_in[3:4, at] / (width * (mean_sq + 1e-06)))
 
 
-def turn(loadings, params):
+def turn(loadings, params, marks, var_index):
     rows, width = loadings.shape
     vmem = pl.BlockSpec(memory_space=pltpu.VMEM)
     return pl.pallas_call(
@@ -128,13 +122,14 @@
         out_shape=(
             jax.ShapeDtypeStruct((rows // BLK, width, BLK), loadings.dtype),
             jax.ShapeDtypeStruct(params.shape, params.dtype),
+            jax.ShapeDtypeStruct((2, *marks.shape), marks.dtype),
         ),
-        in_specs=[vmem, vmem],
-        out_specs=(vmem, vmem),
+        in_specs=[vmem] * 4,
+        out_specs=(vmem, vmem, vmem),
         compiler_params=pltpu.CompilerParams(vmem_limit_bytes=16 << 20),
         cost_estimate=COST,
         name="turn",
-    )(loadings, params)
+    )(loadings, params, marks, jnp.broadcast_to(var_index[None], (8, BLK)))
 
 
 def gathered_from(p, n):
@@ -295,25 +290,34 @@
     while step > 8:
         held = jnp.concatenate([held, swapped(held, step)], axis=0)
         step //= 2
-    prepared = prepare(loadings, threshold, rho, exposure, region, tail_mask, var_index)
-    o8 = swapped(held, 8)
-    o12 = swapped(held, 12)
-    o4 = swapped(held, 4)
-    (o8, o12, o4), prepared = after((o8, o12, o4), prepared)
-    others = [o4, o8, o12]
-    shape = (-1, 1, mine, factors.shape[1])
-    held = jnp.concatenate([x.reshape(shape) for x in (held, *others)], axis=1).reshape(-1, factors.shape[1])
-    loadings, params, where, marks = prepared
-    turned, params = turn(loadings, params)
+    prepared = prepare(threshold, rho, exposure, region, tail_mask)
+    z2 = swapped(held, 8)
+    z3 = swapped(held, 12)
+    z1 = swapped(held, 4)
+    y0 = swapped(held, 2)
+    (z2, z3, z1), prepared = after((z2, z3, z1), prepared)
+
+    def join(*parts):
+        shape = (own.shape[0] // mine, -1, mine, own.shape[1])
+        return jnp.concatenate([x.reshape(shape) for x in parts], axis=1).reshape(-1, own.shape[1])
+
+    own = held
+    rest = join(z1, z2, z3)
+    held = join(own, z1, z2, z3)
+    params, where, marks = prepared
+    held, (var_index, y0) = after(held, (var_index, y0))
+    turned, params, marks = turn(loadings, params, marks, var_index)
     operands = (pattern.T, turned, params, where, marks)
     zero = jnp.zeros((rows // BLK, BLK), jnp.float32)
 
-    across = swapped(held, 2)
+    across = swapped(rest, 2)
     first, turned = after(held, turned)
     beside = swapped(first, 1)
     loss0, sums = weigh(n, 0, operands, (zero, zero), held)
     loss1, sums = weigh(n, 1, operands, sums, beside)
     across, sums = after(across, sums)
+    shape = (own.shape[0] // mine, -1, mine, own.shape[1])
+    across = jnp.concatenate([y0.reshape(shape), across.reshape(shape)], axis=1).reshape(-1, own.shape[1])
     corner = swapped(across, 1)
     loss2, sums = weigh(n, 2, operands, sums, across)
     corner, sums = after(corner, sums)

time: 30 us -> 29.9 us (level)
  starting transfers between devices: 7.88 us -> 9.4 us
  waiting for transfers between devices: 1.98 us -> 1.11 us
  Pallas kernels: 8.41 us -> 7.84 us
    ppermute x6 -> x7, starting transfers between devices: 7.88 us -> 9.4 us  [swapped(): return lax.ppermute(x, 'scen', [(i, i ^ step) for i in range(n)])]
    ppermute x6 -> x7, waiting for transfers between devices: 1.98 us -> 1.11 us  [swapped(): return lax.ppermute(x, 'scen', [(i, i ^ step) for i in range(n)])]
    pallas_call x1, Pallas kernels: 1.68 us -> 1.06 us  [prepare(): pl.pallas_call(prepare_kernel, out_shape=(jax.ShapeDtypeStruct((8, rows),...]
  transfers between devices with their start and end apart: 6 -> 7, of which waited for: 1 -> 1; matrix products, arithmetic and copies ran while one was open for 0% -> 0% of each run, Pallas kernels for 22% -> 20%
where the time goes in v5:
time: 29.9 us; the launch traced here: 29.7 us
  blocking collectives  9.89 us (33%)
  starting transfers between devices  9.4 us (31%)
  Pallas kernels  7.84 us (26%)
  between operations  1.42 us (5%)
  waiting for transfers between devices  1.11 us (4%)
    all_to_all x1, blocking collectives, local(): parts = lax.all_to_all(loss, 'scen', 0, 0)  9.89 us
    ppermute x7, starting transfers between devices, swapped(): return lax.ppermute(x, 'scen', [(i, i ^ step) for i in range(n)])  9.4 us
    pallas_call x4, Pallas kernels, weigh(): pl.pallas_call(functools.partial(weigh_kernel, n, last, bits), out_shape=...  5.23 us
    ppermute x7, waiting for transfers between devices, swapped(): return lax.ppermute(x, 'scen', [(i, i ^ step) for i in range(n)])  1.11 us
    pallas_call x1, Pallas kernels, prepare(): pl.pallas_call(prepare_kernel, out_shape=(jax.ShapeDtypeStruct((8, rows),...  1.06 us
    pallas_call x1, Pallas kernels, turn(): pl.pallas_call(turn_kernel, out_shape=(jax.ShapeDtypeStruct((rows // BLK,...  0.8 us
    pallas_call x1, Pallas kernels, finish(): pl.pallas_call(functools.partial(finish_kernel, factor), out_shape=(jax.S...  0.75 us
  transfers between devices with their start and end apart: 7, of which 1 were waited for; matrix products, arithmetic and copies ran while one was open for 0% of the time, Pallas kernels for 20%

profile of v5, /device:TPU:0, one launch (start us, length us, event | category | flops | bytes accessed | tf_op | source)
XLA Modules:
  0.0 29.7 jit_solution(5800136819483516169)
XLA Ops:
  0.6 4.1 %collective-permute-start = (bf16[16,1024]{1,0:T(8,128)(2,1)}, bf16[16,1024]{1,0:T(8,128)(2,1)S(1)}, u32[]{:S(2)}, u32[]{:S(2)}) collective-permute-start(bf16[16,1024]{1,0:T(8,128)(2,1)} %param.9), channel_id=1, source_target_pairs={{0,8},{1,9},{2,10},{3,11},{4,12},{5,13},{6,14},{7,15},{8,0},{9,1},... | collective-permute-start | bytes 98312 | tf_op jit(solution)/shard_map/ppermute | solution.py:283
  4.7 1.3 %collective-permute-start.1 = (bf16[16,1024]{1,0:T(8,128)(2,1)}, bf16[16,1024]{1,0:T(8,128)(2,1)S(1)}, u32[]{:S(2)}, u32[]{:S(2)}) collective-permute-start(bf16[16,1024]{1,0:T(8,128)(2,1)} %param.9), channel_id=1, source_target_pairs={{0,12},{1,13},{2,14},{3,15},{4,8},{5,9},{6,10},{7,11},{8,4},{9,5},... | collective-permute-start | bytes 98312 | tf_op jit(solution)/shard_map/ppermute | solution.py:283
  6.1 0.2 collective-permute-start.2
  6.3 1.5 %collective-permute-start.3 = (bf16[16,1024]{1,0:T(8,128)(2,1)}, bf16[16,1024]{1,0:T(8,128)(2,1)S(1)}, u32[]{:S(2)}, u32[]{:S(2)}) collective-permute-start(bf16[16,1024]{1,0:T(8,128)(2,1)} %param.9), channel_id=1, source_target_pairs={{0,2},{1,3},{2,0},{3,1},{4,6},{5,7},{6,4},{7,5},{8,10},{9,11},{10,... | collective-permute-start | bytes 98312 | tf_op jit(solution)/shard_map/ppermute | solution.py:283
  7.8 0.0 copy-start.2
  7.8 0.0 copy-start
  7.8 1.1 %prepare.1 = (f32[8,2048]{1,0:T(8,128)S(1)}, bf16[16,2048]{1,0:T(8,128)(2,1)S(1)}, f32[256,128]{1,0:T(8,128)S(1)}) custom-call(f32[1,2048]{1,0:T(1,128)} %bitcast.37, f32[1,2048]{1,0:T(1,128)} %bitcast.38, f32[1,2048]{1,0:T(1,128)} %bitcast.39, s32[1,2048]{1,0:T(1,128)} %bitcast.40, s32[1,256]{1,0:T(1,128)} %bitcast.43), custom_call_target="tpu_custom_call" | custom-call | flops 2000000000 | tf_op jit(solution)/shard_map/prepare/pallas_call | solution.py:72
  9.6 0.0 collective-permute-done
  9.6 1.1 %collective-permute-done.1 = bf16[16,1024]{1,0:T(8,128)(2,1)S(1)} collective-permute-done((bf16[16,1024]{1,0:T(8,128)(2,1)}, bf16[16,1024]{1,0:T(8,128)(2,1)S(1)}, u32[]{:S(2)}, u32[]{:S(2)}) %collective-permute-start.1) | collective-permute-done | bytes 32800 | tf_op jit(solution)/shard_map/ppermute | solution.py:283
  10.7 0.0 collective-permute-done.2
  10.7 1.6 %collective-permute-start.4 = (bf16[48,1024]{1,0:T(8,128)(2,1)S(1)}, bf16[48,1024]{1,0:T(8,128)(2,1)S(1)}, u32[]{:S(2)}, u32[]{:S(2)}) collective-permute-start(bf16[48,1024]{1,0:T(8,128)(2,1)S(1)} %bitcast.33), channel_id=1, source_target_pairs={{0,2},{1,3},{2,0},{3,1},{4,6},{5,7},{6,4},{7,5},{8,10},{9,11},{10,... | collective-permute-start | bytes 294920 | tf_op jit(solution)/shard_map/ppermute | solution.py:283
  12.3 0.0 copy-done.2
  12.3 0.0 collective-permute-done.3
  12.3 0.0 copy-done
  12.3 0.0 copy-start.1
  12.3 0.8 %turn.1 = (bf16[16,512,128]{2,1,0:T(8,128)(2,1)S(1)}, f32[8,2048]{1,0:T(8,128)S(1)}, f32[2,256,128]{2,1,0:T(8,128)S(1)}) custom-call(bf16[2048,512]{1,0:T(8,128)(2,1)S(1)} %copy-done, f32[8,2048]{1,0:T(8,128)S(1)} %get-tuple-element.43.par_in, f32[256,128]{1,0:T(8,128)S(1)} %get-tuple-element.44.mark_in, s32[8,128]{1,0:T(8,128)S(1)} %broadcast_in_dim.32.var_ref), custom_call_target="tpu_custom_call" | custom-call | flops 2000000000 | tf_op jit(solution)/shard_map/turn/pallas_call | solution.py:120
  13.1 0.1 collective-permute-start.5
  13.2 0.0 copy-done.1
  13.2 1.3 %weigh0.1 = (f32[8,128]{1,0:T(8,128)S(1)}, f32[16,128]{1,0:T(8,128)S(1)}, f32[16,128]{1,0:T(8,128)S(1)}) custom-call(s32[4,16]{1,0:T(4,128)S(1)} %bitcast.23, bf16[16,512,128]{2,1,0:T(8,128)(2,1)S(1)} %get-tuple-element.49.refs_1_, f32[8,2048]{1,0:T(8,128)S(1)} %get-tuple-element.50.refs_2_, bf16[16,2048]{1,0:T(8,128)(2,1)S(1)} %get-tuple-element.51.refs_3_, ...), custom_call_target="tpu_custom_call" | custom-call | flops 2000000000 | tf_op jit(solution)/shard_map/weigh0/pallas_call | solution.py:230
  14.6 0.0 collective-permute-done.5.refs_7_
  14.6 1.3 %weigh1.1 = (f32[8,128]{1,0:T(8,128)S(1)}, f32[16,128]{1,0:T(8,128)S(1)}, f32[16,128]{1,0:T(8,128)S(1)}) custom-call(s32[4,16]{1,0:T(4,128)S(1)} %bitcast.24, bf16[16,512,128]{2,1,0:T(8,128)(2,1)S(1)} %get-tuple-element.49.refs_1_, f32[8,2048]{1,0:T(8,128)S(1)} %get-tuple-element.50.refs_2_, bf16[16,2048]{1,0:T(8,128)(2,1)S(1)} %get-tuple-element.51.refs_3_, ...), custom_call_target="tpu_custom_call" | custom-call | flops 2000000000 | tf_op jit(solution)/shard_map/weigh1/pallas_call | solution.py:230
  15.9 0.0 collective-permute-done.4
  15.9 0.5 %collective-permute-start.6 = (bf16[64,1024]{1,0:T(8,128)(2,1)S(1)}, bf16[64,1024]{1,0:T(8,128)(2,1)S(1)}, u32[]{:S(2)}, u32[]{:S(2)}) collective-permute-start(bf16[64,1024]{1,0:T(8,128)(2,1)S(1)} %bitcast.21), channel_id=1, source_target_pairs={{0,1},{1,0},{2,3},{3,2},{4,5},{5,4},{6,7},{7,6},{8,9},{9,8},{10,11... | collective-permute-start | bytes 393224 | tf_op jit(solution)/shard_map/ppermute | solution.py:283
  16.5 1.3 %weigh2.1 = (f32[8,128]{1,0:T(8,128)S(1)}, f32[16,128]{1,0:T(8,128)S(1)}, f32[16,128]{1,0:T(8,128)S(1)}) custom-call(s32[4,16]{1,0:T(4,128)S(1)} %bitcast.25, bf16[16,512,128]{2,1,0:T(8,128)(2,1)S(1)} %get-tuple-element.49.refs_1_, f32[8,2048]{1,0:T(8,128)S(1)} %get-tuple-element.50.refs_2_, bf16[16,2048]{1,0:T(8,128)(2,1)S(1)} %get-tuple-element.51.refs_3_, ...), custom_call_target="tpu_custom_call" | custom-call | flops 2000000000 | tf_op jit(solution)/shard_map/weigh2/pallas_call | solution.py:230
  17.8 0.0 collective-permute-done.6.refs_7_
  17.8 1.3 %weigh3.1 = (f32[16,2,128]{2,1,0:T(2,128)S(1)}, f32[16,128]{1,0:T(8,128)S(1)}, f32[16,128]{1,0:T(8,128)S(1)}) custom-call(s32[4,16]{1,0:T(4,128)S(1)} %bitcast.26, bf16[16,512,128]{2,1,0:T(8,128)(2,1)S(1)} %get-tuple-element.49.refs_1_, f32[8,2048]{1,0:T(8,128)S(1)} %get-tuple-element.50.refs_2_, bf16[16,2048]{1,0:T(8,128)(2,1)S(1)} %get-tuple-element.51.refs_3_, ...), custom_call_target="tpu_custom_call" | custom-call | flops 2000000000 | tf_op jit(solution)/shard_map/weigh3/pallas_call | solution.py:230
  19.1 9.9 %all_to_all.5.parts_ref = f32[16,2,128]{2,1,0:T(2,128)S(1)} all-to-all(f32[16,2,128]{2,1,0:T(2,128)S(1)} %get-tuple-element.71), channel_id=1, replica_groups=mesh['groups'=2,'scen'=16] {'scen'}, dimensions={0} | all-to-all | bytes 32768 | tf_op jit(solution)/shard_map/all_to_all | solution.py:325
  29.0 0.7 %finish.1 = (f32[16,16]{1,0:T(8,128)}, f32[16,128]{1,0:T(8,128)}, f32[16,128]{1,0:T(8,128)}) custom-call(f32[16,2,128]{2,1,0:T(2,128)S(1)} %all_to_all.5.parts_ref, f32[16,128]{1,0:T(8,128)S(1)} %get-tuple-element.72.con_in, f32[16,128]{1,0:T(8,128)S(1)} %get-tuple-element.73.var_in), custom_call_target="tpu_custom_call" | custom-call | tf_op jit(solution)/shard_map/finish/pallas_call | solution.py:267
  (5 shorter events, 0.1 us)
Async XLA Ops:
  0.6 8.9 %collective-permute-start = (bf16[16,1024]{1,0:T(8,128)(2,1)}, bf16[16,1024]{1,0:T(8,128)(2,1)S(1)}, u32[]{:S(2)}, u32[]{:S(2)}) collective-permute-start(bf16[16,1024]{1,0:T(8,128)(2,1)} %param.9), channel_id=1, source_target_pairs={{0,8},{1,9},{2,10},{3,11},{4,12},{5,13},{6,14},{7,15},{8,0},{9,1},... | collective-permute-start | bytes 98312 | tf_op jit(solution)/shard_map/ppermute | solution.py:283
  4.7 5.9 %collective-permute-start.1 = (bf16[16,1024]{1,0:T(8,128)(2,1)}, bf16[16,1024]{1,0:T(8,128)(2,1)S(1)}, u32[]{:S(2)}, u32[]{:S(2)}) collective-permute-start(bf16[16,1024]{1,0:T(8,128)(2,1)} %param.9), channel_id=1, source_target_pairs={{0,12},{1,13},{2,14},{3,15},{4,8},{5,9},{6,10},{7,11},{8,4},{9,5},... | collective-permute-start | bytes 98312 | tf_op jit(solution)/shard_map/ppermute | solution.py:283
  6.1 4.6 %collective-permute-start.2 = (bf16[16,1024]{1,0:T(8,128)(2,1)}, bf16[16,1024]{1,0:T(8,128)(2,1)S(1)}, u32[]{:S(2)}, u32[]{:S(2)}) collective-permute-start(bf16[16,1024]{1,0:T(8,128)(2,1)} %param.9), channel_id=1, source_target_pairs={{0,4},{1,5},{2,6},{3,7},{4,0},{5,1},{6,2},{7,3},{8,12},{9,13},{10,... | collective-permute-start | bytes 98312 | tf_op jit(solution)/shard_map/ppermute | solution.py:283
  6.3 6.0 %collective-permute-start.3 = (bf16[16,1024]{1,0:T(8,128)(2,1)}, bf16[16,1024]{1,0:T(8,128)(2,1)S(1)}, u32[]{:S(2)}, u32[]{:S(2)}) collective-permute-start(bf16[16,1024]{1,0:T(8,128)(2,1)} %param.9), channel_id=1, source_target_pairs={{0,2},{1,3},{2,0},{3,1},{4,6},{5,7},{6,4},{7,5},{8,10},{9,11},{10,... | collective-permute-start | bytes 98312 | tf_op jit(solution)/shard_map/ppermute | solution.py:283
  7.8 4.4 %copy-start.2 = (bf16[16,1024]{1,0:T(8,128)(2,1)S(1)}, bf16[16,1024]{1,0:T(8,128)(2,1)}, u32[]{:S(2)}) copy-start(bf16[16,1024]{1,0:T(8,128)(2,1)} %param.9) | copy-start | bytes 98308
  7.8 4.5 %copy-start = (bf16[2048,512]{1,0:T(8,128)(2,1)S(1)}, bf16[2048,512]{1,0:T(8,128)(2,1)}, u32[]{:S(2)}) copy-start(bf16[2048,512]{1,0:T(8,128)(2,1)} %load_ref.1) | copy-start | bytes 6291460
  10.7 5.2 %collective-permute-start.4 = (bf16[48,1024]{1,0:T(8,128)(2,1)S(1)}, bf16[48,1024]{1,0:T(8,128)(2,1)S(1)}, u32[]{:S(2)}, u32[]{:S(2)}) collective-permute-start(bf16[48,1024]{1,0:T(8,128)(2,1)S(1)} %bitcast.33), channel_id=1, source_target_pairs={{0,2},{1,3},{2,0},{3,1},{4,6},{5,7},{6,4},{7,5},{8,10},{9,11},{10,... | collective-permute-start | bytes 294920 | tf_op jit(solution)/shard_map/ppermute | solution.py:283
  12.3 0.9 %copy-start.1 = (s32[16,4]{0,1:T(4,128)S(1)}, s32[16,4]{0,1:T(4,128)}, u32[]{:S(2)}) copy-start(s32[16,4]{0,1:T(4,128)} %param.11) | copy-start | bytes 772
  13.1 1.4 %collective-permute-start.5 = (bf16[64,1024]{1,0:T(8,128)(2,1)S(1)}, bf16[64,1024]{1,0:T(8,128)(2,1)S(1)}, u32[]{:S(2)}, u32[]{:S(2)}) collective-permute-start(bf16[64,1024]{1,0:T(8,128)(2,1)S(1)} %bitcast.19), channel_id=1, source_target_pairs={{0,1},{1,0},{2,3},{3,2},{4,5},{5,4},{6,7},{7,6},{8,9},{9,8},{10,11... | collective-permute-start | bytes 393224 | tf_op jit(solution)/shard_map/ppermute | solution.py:283
  15.9 1.9 %collective-permute-start.6 = (bf16[64,1024]{1,0:T(8,128)(2,1)S(1)}, bf16[64,1024]{1,0:T(8,128)(2,1)S(1)}, u32[]{:S(2)}, u32[]{:S(2)}) collective-permute-start(bf16[64,1024]{1,0:T(8,128)(2,1)S(1)} %bitcast.21), channel_id=1, source_target_pairs={{0,1},{1,0},{2,3},{3,2},{4,5},{5,4},{6,7},{7,6},{8,9},{9,8},{10,11... | collective-permute-start | bytes 393224 | tf_op jit(solution)/shard_map/ppermute | solution.py:283
